TPU v7x, 128 devices: a whole 4x4x4 slice. The times are simulated.
128 devices in a mesh: gx: 16 (over y, z), gy: 8 (over x, core).
Axes of the slice: x: 4, y: 4, z: 4, core: 2. Of those that a mesh axis runs over, the one named last changes fastest.
Arguments:
- queries: bfloat16 [1024, 16384], P('gy', 'gx'), may hold values from -200 to 200, as said below
- keys: bfloat16 [1024, 1024], P('gy'), may hold values from -8 to 8, as said below
- values: bfloat16 [1024, 1024], P('gy'), may hold values from -6 to 6
- lengths: int32 [8], P('gy'), may hold values from 1 to 128, 768 in all
- offsets: int32 [8], P('gy'), may hold values from 0 to 63
- resid_in: bfloat16 [1024, 16384], P('gx', 'gy'), may hold values from -8 to 8, as said below
- w_out: bfloat16 [16384, 16384], P('gx', 'gy'), may hold values from -0.1875 to 0.1875
- norm_gain: bfloat16 [16384], P('gy'), may hold values from 0.5 to 1.5
- w_gate: bfloat16 [16384, 26624], P('gy', 'gx'), may hold values from -0.046875 to 0.046875
- w_up: bfloat16 [16384, 26624], P('gy', 'gx'), may hold values from -0.046875 to 0.046875
- w_down: bfloat16 [26624, 16384], P('gx', 'gy'), may hold values from -0.0390625 to 0.0390625
Outputs:
- layer_out: bfloat16 [1024, 16384], P('gx', 'gy')
Inputs may be any that keep to these rules, and one draw needn't show every extreme that they name: queries: some rows may lie along keys of their own sequence. keys are of order one. `resid_in`: entries are of order one.
All inputs are finite; a program needn't handle non-finite values. No bound on the sum of `lengths` on one device may be relied on, other than what follows from the above.
Results may differ from a plain program's by a relative error of at most 0.0055.
Values may be sent and summed in bfloat16 or wider, within the bound.
No kernel may reach another device: no remote copies, remote signals or barrier semaphores. Data moves between devices by JAX's collectives and lax.ppermute only.
A program may use at most 128 MiB of HBM per device.

v0:
```python
import jax
import jax.numpy as jnp
from jax import lax
from jax.sharding import PartitionSpec as P

D = 16384
QUERY_HEADS = 128
KEY_VALUE_HEADS = 8
HEAD_SIZE = 128
SEQUENCE_SLOTS = 128


def attend_local(queries, keys, values, lengths, offsets):
    seqs = lengths.shape[0]
    local_heads = queries.shape[1] // HEAD_SIZE
    query_group = QUERY_HEADS // KEY_VALUE_HEADS
    head = lax.axis_index("gx") * local_heads // query_group
    key_one = lax.dynamic_slice_in_dim(keys, head * HEAD_SIZE, HEAD_SIZE, 1).reshape(
        seqs, SEQUENCE_SLOTS, HEAD_SIZE
    )
    value_one = lax.dynamic_slice_in_dim(values, head * HEAD_SIZE, HEAD_SIZE, 1).reshape(
        seqs, SEQUENCE_SLOTS, HEAD_SIZE
    )
    query_all = queries.reshape(seqs, SEQUENCE_SLOTS, local_heads, HEAD_SIZE)
    scores = jnp.einsum("sqhd,skd->shqk", query_all, key_one, preferred_element_type=jnp.float32)
    scores = scores / jnp.sqrt(jnp.float32(HEAD_SIZE))
    place = jnp.arange(SEQUENCE_SLOTS, dtype=jnp.int32)
    rows = place[None, :, None]
    cols = place[None, None, :]
    inside = (cols >= offsets[:, None, None]) & (cols < lengths[:, None, None]) & (cols <= rows)
    visible = (inside | (cols == rows))[:, None, :, :]
    scores = jnp.where(visible, scores, jnp.float32(-1e30))
    top = jnp.max(scores, axis=-1, keepdims=True)
    expo = jnp.where(visible, jnp.exp(scores - top), jnp.float32(0.0))
    probs = (expo / jnp.sum(expo, axis=-1, keepdims=True)).astype(jnp.bfloat16)
    attn = jnp.einsum("shqk,skd->sqhd", probs, value_one, preferred_element_type=jnp.float32)
    return attn.astype(jnp.bfloat16).reshape(seqs * SEQUENCE_SLOTS, local_heads * HEAD_SIZE)


def per_device(
    queries, keys, values, lengths, offsets, resid_in, w_out, norm_gain, w_gate, w_up, w_down
):
    attn = attend_local(queries, keys, values, lengths, offsets)
    gathered = lax.all_gather(attn, "gy", axis=0, tiled=True)
    block = gathered
    attn_proj = lax.psum_scatter(
        jnp.dot(block, w_out, preferred_element_type=jnp.float32),
        "gx",
        scatter_dimension=0,
        tiled=True,
    )
    resid = (resid_in.astype(jnp.float32) + attn_proj).astype(jnp.bfloat16)
    wide = resid.astype(jnp.float32)
    squares = lax.psum(jnp.sum(wide * wide, axis=1), "gy")
    scale = lax.rsqrt(squares / D + 1e-05)
    normed = (wide * scale[:, None] * norm_gain.astype(jnp.float32)[None, :]).astype(jnp.bfloat16)
    full_rows = lax.all_gather(normed, "gx", axis=0, tiled=True)
    units = w_gate.shape[1]
    block = full_rows
    gate_block = jnp.dot(block, w_gate, preferred_element_type=jnp.float32)
    up_block = jnp.dot(block, w_up, preferred_element_type=jnp.float32)
    both = lax.psum_scatter(
        jnp.concatenate([gate_block, up_block], axis=1), "gy", scatter_dimension=0, tiled=True
    )
    hidden = (jax.nn.silu(both[:, :units]) * both[:, units:]).astype(jnp.bfloat16)
    hidden_all = lax.all_gather(hidden, "gy", axis=0, tiled=True)
    block = hidden_all
    mixed = lax.psum_scatter(
        jnp.dot(block, w_down, preferred_element_type=jnp.float32),
        "gx",
        scatter_dimension=0,
        tiled=True,
    )
    return (wide + mixed).astype(jnp.bfloat16)


def solution(mesh):
    in_specs = (
        P("gy", "gx"),
        P("gy", None),
        P("gy", None),
        P("gy"),
        P("gy"),
        P("gx", "gy"),
        P("gx", "gy"),
        P("gy"),
        P("gy", "gx"),
        P("gy", "gx"),
        P("gx", "gy"),
    )
    out_specs = P("gx", "gy")
    return jax.shard_map(
        per_device, mesh=mesh, in_specs=in_specs, out_specs=out_specs, check_vma=False
    )
```

profile of v0, /device:TPU:0, one launch (start us, length us, event | category | flops | bytes accessed | tf_op | source)
XLA Modules:
  0.0 444.3 jit_solution(2492054579517186283)
XLA Ops:
  7.9 0.1 fusion.13
  8.0 1.2 fusion.21
  9.2 0.1 fusion.7
  9.3 1.8 convolution_convert_fusion
  11.1 0.0 all-gather.4.cloned.1.call-update
  11.1 0.0 reduce-scatter.4.cloned.1.call-start
  11.1 29.8 %all-gather.4.cloned.1.call-done = bf16[1024,1024]{0,1:T(8,128)(2,1)} async-done(((bf16[128,1024]{0,1:T(8,128)(2,1)}), bf16[1024,1024]{0,1:T(8,128)(2,1)}) %all-gather.4.cloned.1.call-update) | async-done | bytes 2097168 | tf_op jit(solution)/shard_map/all_gather | solution.py:44
  40.9 10.6 %fusion.22 = f32[1024,2048]{1,0:T(8,128)} fusion(bf16[1024,1024]{0,1:T(8,128)(2,1)} %all-gather.4.cloned.1.call-done, bf16[1024,2048]{1,0:T(8,128)(2,1)} %param.17), kind=kOutput, calls=%fused_computation.36 | convolution fusion | flops 4294967296 | bytes 14680064 | tf_op jit(solution)/shard_map/dot_general | solution.py:47
  51.5 0.0 reduce-scatter.4.cloned.1.call-update
  51.6 0.0 all-gather.6.cloned.1.call-start
  51.6 0.6 copy-done.3
  52.2 85.6 %reduce-scatter.4.cloned.1.call-done = f32[64,2048]{1,0:T(8,128)} async-done(((f32[1024,2048]{1,0:T(8,128)}), f32[64,2048]{1,0:T(8,128)}) %reduce-scatter.4.cloned.1.call-update) | async-done | bytes 524304 | tf_op jit(solution)/shard_map/reduce_scatter | solution.py:46
  137.9 1.2 fusion.3
  139.1 13.2 %psum.7 = f32[64]{0:T(128)S(1)} all-reduce(f32[64]{0:T(128)S(1)} %get-tuple-element.5), channel_id=1, replica_groups=mesh['gx'=16,'gy'=8] {'gy'}, use_global_device_ids=true, to_apply=%region_4.5 | all-reduce | flops 64 | bytes 512 | tf_op jit(solution)/shard_map/psum | solution.py:54
  152.3 0.8 fusion.5
  153.2 0.0 all-gather.6.cloned.1.call-update
  153.2 0.2 reduce-scatter.6.cloned.1.call-start
  153.4 48.4 %all-gather.6.cloned.1.call-done = bf16[1024,2048]{1,0:T(8,128)(2,1)} async-done(((bf16[64,2048]{1,0:T(8,128)(2,1)}), bf16[1024,2048]{1,0:T(8,128)(2,1)}) %all-gather.6.cloned.1.call-update) | async-done | bytes 4194320 | tf_op jit(solution)/shard_map/all_gather | solution.py:57
  201.8 11.6 %fusion.24 = f32[1024,1664]{1,0:T(8,128)S(1)} fusion(bf16[1024,2048]{1,0:T(8,128)(2,1)} %all-gather.6.cloned.1.call-done, bf16[2048,1664]{1,0:T(8,128)(2,1)} %param.20), kind=kOutput, calls=%fused_computation.38 | convolution fusion | flops 6979321856 | bytes 17825792 | tf_op jit(solution)/shard_map/dot_general | solution.py:61
  213.5 10.7 %fusion.23 = f32[1024,1664]{1,0:T(8,128)S(1)} fusion(bf16[1024,2048]{1,0:T(8,128)(2,1)S(1)} %copy-done.4, bf16[2048,1664]{1,0:T(8,128)(2,1)} %param.19), kind=kOutput, calls=%fused_computation.37 | convolution fusion | flops 6979321856 | bytes 17825792 | tf_op jit(solution)/shard_map/dot_general | solution.py:60
  224.1 5.2 %pad_maximum_fusion = f32[1024,3328]{1,0:T(8,128)} fusion(f32[1024,1664]{1,0:T(8,128)S(1)} %fusion.24, f32[1024,1664]{1,0:T(8,128)S(1)} %fusion.23), kind=kLoop, calls=%fused_computation | loop fusion | flops 3407872 | bytes 27262976 | tf_op jit(solution)/shard_map/concatenate | solution.py:63
  229.4 0.0 reduce-scatter.6.cloned.1.call-update
  229.4 0.0 all-gather.8.cloned.1.call-start
  229.4 77.0 %reduce-scatter.6.cloned.1.call-done = f32[128,3328]{1,0:T(8,128)} async-done(((f32[1024,3328]{1,0:T(8,128)}), f32[128,3328]{1,0:T(8,128)}) %reduce-scatter.6.cloned.1.call-update) | async-done | bytes 1703952 | tf_op jit(solution)/shard_map/reduce_scatter | solution.py:62
  306.5 2.4 fusion.2
  308.9 0.0 all-gather.8.cloned.1.call-update
  308.9 0.0 reduce-scatter.8.cloned.1.call-start
  308.9 28.5 %all-gather.8.cloned.1.call-done = bf16[1024,1664]{1,0:T(8,128)(2,1)} async-done(((bf16[128,1664]{1,0:T(8,128)(2,1)}), bf16[1024,1664]{1,0:T(8,128)(2,1)}) %all-gather.8.cloned.1.call-update) | async-done | bytes 3407888 | tf_op jit(solution)/shard_map/all_gather | solution.py:66
  337.5 13.0 %fusion.25 = f32[1024,2048]{1,0:T(8,128)} fusion(bf16[1024,1664]{1,0:T(8,128)(2,1)} %all-gather.8.cloned.1.call-done, bf16[1664,2048]{1,0:T(8,128)(2,1)} %param.21), kind=kOutput, calls=%fused_computation.39 | convolution fusion | flops 6979321856 | bytes 18612224 | tf_op jit(solution)/shard_map/dot_general | solution.py:69
  350.5 0.0 reduce-scatter.8.cloned.1.call-update
  350.5 85.1 %reduce-scatter.8.cloned.1.call-done = f32[64,2048]{1,0:T(8,128)} async-done(((f32[1024,2048]{1,0:T(8,128)}), f32[64,2048]{1,0:T(8,128)}) %reduce-scatter.8.cloned.1.call-update) | async-done | bytes 524304 | tf_op jit(solution)/shard_map/reduce_scatter | solution.py:68
  435.6 1.8 fusion.6
  (13 shorter events, 0.0 us)
Async XLA Ops:
  6.5 1.5 copy-start
  6.5 34.4 %all-gather.4.cloned.1.call-start = ((), (), s32[]{:S(2)}) async-start(), calls=%async_computation.3 | async-start | bytes 2359296 | tf_op jit(solution)/shard_map/all_gather | solution.py:44
  11.1 126.8 %reduce-scatter.4.cloned.1.call-start = ((), (), s32[]{:S(2)}) async-start(), calls=%async_computation.4 | async-start | bytes 8912896 | tf_op jit(solution)/shard_map/reduce_scatter | solution.py:46
  51.5 0.7 copy-start.3
  51.5 86.3 %copy-start.2 = (bf16[64,2048]{1,0:T(8,128)(2,1)S(1)}, bf16[64,2048]{1,0:T(8,128)(2,1)}, u32[]{:S(2)}) copy-start(bf16[64,2048]{1,0:T(8,128)(2,1)} %param.16) | copy-start | bytes 786436
  51.6 150.2 %all-gather.6.cloned.1.call-start = ((), (), s32[]{:S(2)}) async-start(), calls=%async_computation.5 | async-start | bytes 4456448 | tf_op jit(solution)/shard_map/all_gather | solution.py:57
  153.2 153.3 %reduce-scatter.6.cloned.1.call-start = ((), (), s32[]{:S(2)}) async-start(), calls=%async_computation.6 | async-start | bytes 15335424 | tf_op jit(solution)/shard_map/reduce_scatter | solution.py:62
  201.8 11.6 %copy-start.4 = (bf16[1024,2048]{1,0:T(8,128)(2,1)S(1)}, bf16[1024,2048]{1,0:T(8,128)(2,1)}, u32[]{:S(2)}) copy-start(bf16[1024,2048]{1,0:T(8,128)(2,1)} %all-gather.6.cloned.1.call-done) | copy-start | bytes 12582916
  229.4 108.1 %all-gather.8.cloned.1.call-start = ((), (), s32[]{:S(2)}) async-start(), calls=%async_computation.7 | async-start | bytes 3833856 | tf_op jit(solution)/shard_map/all_gather | solution.py:66
  308.9 126.7 %reduce-scatter.8.cloned.1.call-start = ((), (), s32[]{:S(2)}) async-start(), calls=%async_computation.8 | async-start | bytes 8912896 | tf_op jit(solution)/shard_map/reduce_scatter | solution.py:68
  337.5 99.9 %copy-start.1 = (bf16[128,1024]{1,0:T(8,128)(2,1)S(1)}, bf16[128,1024]{1,0:T(8,128)(2,1)}, u32[]{:S(2)}) copy-start(bf16[128,1024]{1,0:T(8,128)(2,1)} %param.12) | copy-start | bytes 786436
Sparse Core Ops, SparseCore 0:
  11.2 29.6 all-gather.3
  51.7 86.1 reduce-scatter.3
  153.3 48.4 all-gather.5
  229.5 76.8 reduce-scatter.5
  309.0 28.4 all-gather.7
  350.7 84.9 reduce-scatter.7
where the time goes:
time: 445 us; the launch traced here: 444 us
  waiting for transfers between devices  355 us (80%)
  matrix products  48.9 us (11%)
  between operations  14.9 us (3%)
  blocking collectives  13.2 us (3%)
  other arithmetic  11.7 us (3%)
    reduce_scatter x1, waiting for transfers between devices, per_device(): lax.psum_scatter(jnp.dot(block, w_out, preferred_element_type=jnp.float32...  85.6 us
    reduce_scatter x1, waiting for transfers between devices, per_device(): lax.psum_scatter(jnp.dot(block, w_down, preferred_element_type=jnp.float3...  85.1 us
    reduce_scatter x1, waiting for transfers between devices, per_device(): lax.psum_scatter(jnp.concatenate([gate_block, up_block], axis=1), 'gy', s...  77 us
    all_gather x1, waiting for transfers between devices, per_device(): full_rows = lax.all_gather(normed, 'gx', axis=0, tiled=True)  48.4 us
    all_gather x1, waiting for transfers between devices, per_device(): gathered = lax.all_gather(attn, 'gy', axis=0, tiled=True)  29.8 us
    all_gather x1, waiting for transfers between devices, per_device(): hidden_all = lax.all_gather(hidden, 'gy', axis=0, tiled=True)  28.5 us
    psum x1, blocking collectives, per_device(): squares = lax.psum(jnp.sum(wide * wide, axis=1), 'gy')  13.2 us
    dot_general x1, matrix products, per_device(): jnp.dot(block, w_down, preferred_element_type=jnp.float32)  13 us
  transfers between devices with their start and end apart: 6, of which 6 were waited for; matrix products, arithmetic and copies ran while one was open for 0% of the time, Pallas kernels for 0%

commit v1 on v0

v1 whole, which is shorter than its diff:
```python
import jax
import jax.numpy as jnp
from jax import lax
from jax.experimental import pallas as pl
from jax.experimental.pallas import tpu as pltpu
from jax.sharding import PartitionSpec as P

D = 16384
QUERY_HEADS = 128
KEY_VALUE_HEADS = 8
HEAD_SIZE = 128
SEQUENCE_SLOTS = 128
SIDE = 4
TILE = 256
AHEAD = 6
VMEM_BYTES = 52 * 1024 * 1024
BF16 = jnp.bfloat16
F32 = jnp.float32

BOTH = ("gx", "gy")
CORES = [[2 * x, 2 * x + 1] for x in range(SIDE)]
SWAP = [(2 * x + c, 2 * x + 1 - c) for x in range(SIDE) for c in range(2)]


def across(major, mask):
    pairs = []
    for place in range(16):
        for spot in range(8):
            flip = mask if (spot % 2 == 0) == major else 4 * mask
            pairs.append((8 * place + spot, 8 * (place ^ flip) + spot))
    return pairs


def across_x(masks):
    return [(spot, spot ^ (2 * masks[spot % 2])) for spot in range(8)]


def attend_local(queries, keys, values, lengths, offsets):
    seqs = lengths.shape[0]
    local_heads = queries.shape[1] // HEAD_SIZE
    query_group = QUERY_HEADS // KEY_VALUE_HEADS
    head = lax.axis_index("gx") * local_heads // query_group
    key_one = lax.dynamic_slice_in_dim(keys, head * HEAD_SIZE, HEAD_SIZE, 1).reshape(
        seqs, SEQUENCE_SLOTS, HEAD_SIZE
    )
    value_one = lax.dynamic_slice_in_dim(values, head * HEAD_SIZE, HEAD_SIZE, 1).reshape(
        seqs, SEQUENCE_SLOTS, HEAD_SIZE
    )
    query_all = queries.reshape(seqs, SEQUENCE_SLOTS, local_heads, HEAD_SIZE)
    scores = jnp.einsum("sqhd,skd->shqk", query_all, key_one, preferred_element_type=F32)
    scores = scores / jnp.sqrt(F32(HEAD_SIZE))
    place = jnp.arange(SEQUENCE_SLOTS, dtype=jnp.int32)
    rows = place[None, :, None]
    cols = place[None, None, :]
    inside = (cols >= offsets[:, None, None]) & (cols < lengths[:, None, None]) & (cols <= rows)
    visible = (inside | (cols == rows))[:, None, :, :]
    scores = jnp.where(visible, scores, F32(-1e30))
    top = jnp.max(scores, axis=-1, keepdims=True)
    expo = jnp.where(visible, jnp.exp(scores - top), F32(0.0))
    probs = (expo / jnp.sum(expo, axis=-1, keepdims=True)).astype(BF16)
    attn = jnp.einsum("shqk,skd->sqhd", probs, value_one, preferred_element_type=F32)
    return attn.astype(BF16).reshape(seqs * SEQUENCE_SLOTS, local_heads * HEAD_SIZE)


def pick(array, index, axis=0):
    return lax.dynamic_index_in_dim(array, index, axis, keepdims=False)


def add_up(blocks):
    total = blocks[0].astype(F32)
    for block in blocks[1:]:
        total = total + block.astype(F32)
    return total


def move(array, major, mask):
    return lax.ppermute(array, BOTH, across(major, mask))


def sum_major(blocks, size):
    blocks = [blocks[0]] + [move(blocks[e], True, e) for e in (2, 1, 3)]
    return [add_up([block[q * size : (q + 1) * size] for block in blocks]) for q in range(SIDE)]


def gather_x(block):
    other = lax.ppermute(block, "gy", across_x((1, 3)))
    return [block, other, lax.ppermute(jnp.concatenate([block, other]), "gy", across_x((3, 1)))]


def halves(core, array, axis=0):
    return pick(array, core, axis), pick(array, 1 - core, axis)


def swap(array):
    return lax.ppermute(array, "gy", SWAP)


def in_three(sums):
    lanes = []
    for _ in range(3):
        rounded = lax.reduce_precision(sums, 8, 7)
        lanes.append(rounded.astype(BF16))
        sums = sums - rounded
    return jnp.pad(jnp.stack(lanes, axis=1), ((0, 0), (0, 128 - 3)))


def after(array, *earlier):
    return lax.optimization_barrier((array, earlier))[0]


SMEM = pl.BlockSpec(memory_space=pltpu.SMEM)
VMEM = pl.BlockSpec(memory_space=pltpu.VMEM)
HBM = pl.BlockSpec(memory_space=pltpu.HBM)


def fill(places, given, lhs, size):
    i = 0
    for ref in given:
        for row in range(0, ref.shape[0], size):
            at = pl.multiple_of(places[i] * size, size)
            lhs[pl.ds(at, size), :] = ref[row : row + size, :]
            i += 1


def project(places, size, blocks, weight):
    depth, width = weight.shape
    rows = size * places.shape[0]
    tiles = width // TILE

    def kernel(places, *refs):
        given, weight_ref, outs = refs[: len(blocks)], refs[-8], refs[-7:-3]
        lhs, tile_refs, sems = refs[-3:]

        def copy(j):
            at = pl.ds(pl.multiple_of(j * TILE, TILE), TILE)
            return pltpu.make_async_copy(weight_ref.at[:, at], tile_refs.at[j], sems.at[j])

        for j in range(tiles):
            copy(j).start()
        fill(places, given, lhs, size)

        @pl.loop(0, tiles)
        def _(j):
            copy(j).wait()
            product = jnp.dot(lhs[...], tile_refs[j], preferred_element_type=F32).astype(BF16)
            at = pl.ds(pl.multiple_of(j * TILE, TILE), TILE)
            for e in range(4):
                outs[e][:, at] = product[e * rows // 4 : (e + 1) * rows // 4]

    return pl.pallas_call(
        kernel,
        in_specs=[SMEM] + [VMEM] * len(blocks) + [HBM],
        out_specs=[VMEM] * 4,
        scratch_shapes=[
            pltpu.VMEM((rows, depth), BF16),
            pltpu.VMEM((tiles, depth, TILE), BF16),
            pltpu.SemaphoreType.DMA((tiles,)),
        ],
        out_shape=[jax.ShapeDtypeStruct((rows // 4, width), BF16)] * 4,
        compiler_params=pltpu.CompilerParams(vmem_limit_bytes=VMEM_BYTES),
        cost_estimate=pl.CostEstimate(
            flops=2 * rows * depth * width, bytes_accessed=2 * depth * width, transcendentals=0
        ),
    )(places, *blocks, weight)


def gate_and_up(places, blocks, w_gate, w_up):
    depth, units = w_gate.shape
    rows = blocks[0].shape[0]
    full = units // TILE
    rest = units - full * TILE

    def kernel(places, *refs):
        given, gate_ref, up_ref, outs = refs[:4], refs[4], refs[5], refs[6:8]
        lhs, tile_refs, sems = refs[8:]

        def copy(weight_ref, j, first):
            at = pl.ds(pl.multiple_of(j * TILE, TILE), TILE)
            return pltpu.make_async_copy(
                weight_ref.at[:, at], tile_refs.at[first + j], sems.at[first + j]
            )

        def copy_rest(weight_ref, i):
            return pltpu.make_async_copy(
                weight_ref.at[:, pl.ds(full * TILE, rest)],
                tile_refs.at[2 * full, :, pl.ds(i * rest, rest)],
                sems.at[2 * full + i],
            )

        def store(product, at):
            for i in range(2):
                outs[i][:, at] = product[2 * i * rows : 2 * (i + 1) * rows]

        def multiply(tile):
            return jnp.dot(lhs[:, :depth], tile, preferred_element_type=F32).astype(BF16)

        for j in range(AHEAD):
            copy(gate_ref, j, 0).start()
        fill(places, given, lhs, rows)
        store(lhs[:, depth:], pl.ds(2 * units, 128))

        @pl.loop(0, full)
        def _(j):
            copy(gate_ref, j, 0).wait()

            @pl.when(j + AHEAD < full)
            def _():
                copy(gate_ref, j + AHEAD, 0).start()

            @pl.when(j + AHEAD >= full)
            def _():
                copy(up_ref, j + AHEAD - full, full).start()

            at = pl.multiple_of(j * TILE, TILE)
            store(multiply(tile_refs[j]), pl.ds(at, TILE))

        @pl.loop(0, full)
        def _(j):
            copy(up_ref, j, full).wait()

            @pl.when(j + AHEAD < full)
            def _():
                copy(up_ref, j + AHEAD, full).start()

            @pl.when(j + AHEAD == full)
            def _():
                copy_rest(gate_ref, 0).start()
                copy_rest(up_ref, 1).start()

            at = pl.multiple_of(units + j * TILE, 128)
            store(multiply(tile_refs[full + j]), pl.ds(at, TILE))

        copy_rest(gate_ref, 0).wait()
        copy_rest(up_ref, 1).wait()
        product = multiply(tile_refs[2 * full])
        store(product[:, :rest], pl.ds(full * TILE, rest))
        store(product[:, rest:], pl.ds(units + full * TILE, rest))

    return pl.pallas_call(
        kernel,
        in_specs=[SMEM] + [VMEM] * 4 + [HBM] * 2,
        out_specs=[VMEM] * 2,
        scratch_shapes=[
            pltpu.VMEM((4 * rows, depth + 128), BF16),
            pltpu.VMEM((2 * full + 1, depth, TILE), BF16),
            pltpu.SemaphoreType.DMA((2 * full + 2,)),
        ],
        out_shape=[jax.ShapeDtypeStruct((2 * rows, 2 * units + 128), BF16)] * 2,
        compiler_params=pltpu.CompilerParams(vmem_limit_bytes=VMEM_BYTES),
        cost_estimate=pl.CostEstimate(
            flops=16 * rows * depth * units, bytes_accessed=4 * depth * units, transcendentals=0
        ),
    )(places, *blocks, w_gate, w_up)


def sum_over_x(sent, kept, earlier):
    rows = sent.shape[0] // 2
    arrived = lax.ppermute(sent, "gy", across_x((3, 1)))
    other = (kept[rows:].astype(F32) + arrived[rows:].astype(F32)).astype(BF16)
    if earlier is not None:
        other = after(other, earlier)
    other = lax.ppermute(other, "gy", across_x((1, 3)))
    return add_up([kept[:rows], arrived[:rows], other])


def per_device(
    queries, keys, values, lengths, offsets, resid_in, w_out, norm_gain, w_gate, w_up, w_down
):
    place = lax.axis_index("gx")
    y, z = place // SIDE, place % SIDE
    x, core = lax.axis_index("gy") // 2, lax.axis_index("gy") % 2
    here, there = jnp.where(core == 0, z, y), jnp.where(core == 0, y, z)
    rows, columns = resid_in.shape
    half = rows // 2
    units = w_gate.shape[1]
    four = jnp.arange(SIDE, dtype=jnp.int32)
    two = jnp.arange(2, dtype=jnp.int32)
    cores = jnp.stack([core, 1 - core])

    w_gate = lax.all_gather(w_gate, "gy", axis=0, tiled=True, axis_index_groups=CORES)
    w_up = lax.all_gather(w_up, "gy", axis=0, tiled=True, axis_index_groups=CORES)

    mine = attend_local(queries, keys, values, lengths, offsets)
    mine = gather_x(mine)
    theirs = swap(jnp.concatenate(mine))
    near = jnp.where(core == 0, 1, 3)
    zero, far = jnp.zeros_like(near), jnp.full_like(near, 2)
    lines = x ^ jnp.stack(
        [
            jnp.stack([zero, near, 4 - near, far]),
            jnp.stack([zero, 4 - near, near, far]),
        ]
    )
    in_y = (lines ^ y)[:, :, None]
    in_z = ((2 * cores[:, None] + two[None, :]) ^ z)[:, None, :]
    places = jnp.where(core == 0, 4 * in_z + in_y, 4 * in_y + in_z).reshape(16)
    parts = sum_major(project(places, rows, mine + [theirs], w_out), rows)
    arrived = [move(parts[q].astype(BF16), False, q) for q in (2, 1, 3)]
    attn_proj = add_up([parts[0]] + arrived)
    wide = (resid_in.astype(F32) + attn_proj).astype(BF16).astype(F32)
    squares = in_three(jnp.sum(wide * wide, axis=1))
    scaled = jnp.concatenate([(wide * norm_gain.astype(F32)).astype(BF16), squares], axis=1)
    mine, theirs = halves(core, scaled.reshape(2, half, -1))
    theirs = swap(theirs)
    first, second = jnp.where(core == 0, mine, theirs), jnp.where(core == 0, theirs, mine)
    squares = mine[:, columns:].astype(F32) + theirs[:, columns:].astype(F32)
    scaled = jnp.concatenate(
        [first[:, :columns], second[:, :columns], in_three(jnp.sum(squares, axis=1))], axis=1
    )
    scaled = [scaled] + [move(scaled, False, q) for q in (1, 2, 3)]

    quarter = half // 2
    outs, hidden = [], None
    for chunk in range(2):
        taken = slice(chunk * quarter, (chunk + 1) * quarter)
        block = jnp.concatenate([block[taken] for block in scaled])
        blocks = [block] + [move(block, True, e) for e in (1, 2, 3)]
        slot = x ^ here ^ four
        slots = jnp.where(slot == 4 - near, 0, jnp.where(slot == 2, 1, jnp.where(slot == 0, 2, 3)))
        both = sum_over_x(*gate_and_up(slots, blocks, w_gate, w_up), hidden)
        scale = lax.rsqrt(jnp.sum(both[:, 2 * units :], axis=1, keepdims=True) / D + 1e-05)
        gate, up = both[:, :units] * scale, both[:, units : 2 * units] * scale
        hidden = (jax.nn.silu(gate) * up).astype(BF16)
        mine = gather_x(hidden)
        if chunk:
            mine = after(mine, *products)
        theirs = swap(jnp.concatenate(mine))
        ours = 4 * (lines[0] ^ here)[:, None] + four[None, :]
        others = (lines[1] ^ there)[:, None] + 4 * four[None, :]
        places = jnp.stack([2 * ours + core, 2 * others + 1 - core]).reshape(32)
        products = project(places, quarter, mine + [theirs], w_down)
        parts = sum_major(products, half)
        arrived = [move(parts[q].astype(BF16), False, q) for q in (2, 1, 3)]
        own = wide.reshape(2, 2, quarter, columns)[:, chunk].reshape(half, columns)
        outs.append((own + add_up([parts[0]] + arrived)).astype(BF16).reshape(2, quarter, columns))
    return jnp.stack(outs, axis=1).reshape(rows, columns)


def solution(mesh):
    in_specs = (
        P("gy", "gx"),
        P("gy", None),
        P("gy", None),
        P("gy"),
        P("gy"),
        P("gx", "gy"),
        P("gx", "gy"),
        P("gy"),
        P("gy", "gx"),
        P("gy", "gx"),
        P("gx", "gy"),
    )
    out_specs = P("gx", "gy")
    return jax.shard_map(
        per_device, mesh=mesh, in_specs=in_specs, out_specs=out_specs, check_vma=False
    )
```

time: 445 us -> 255 us (0.57)
  waiting for transfers between devices: 355 us -> 112 us
  starting transfers between devices: 0.39 us -> 56.1 us
  Pallas kernels: 0 us -> 53.8 us
  matrix products: 48.9 us -> 1.29 us
  blocking collectives: 13.2 us -> 0 us
  local copies, waits for them, and re-layouts: 0.63 us -> 5.86 us
    reduce_scatter x3 -> x0, waiting for transfers between devices: 248 us -> none  [the longest x1 85.6 us: per_device(): lax.psum_scatter(jnp.dot(block, w_out, preferred_element_type=jnp.float32...]
    ppermute x0 -> x41, waiting for transfers between devices: none -> 110 us  [the longest x27 62.3 us: move(): return lax.ppermute(array, BOTH, across(major, mask))]
    all_gather x3 -> x2, waiting for transfers between devices: 107 us -> 0.01 us  [the longest x1 0.01 us: per_device(): lax.all_gather(w_gate, 'gy', axis=0, tiled=True, axis_index_groups=CORES)]
    ppermute x0 -> x41, starting transfers between devices: none -> 56.1 us  [the longest x27 39.7 us: move(): return lax.ppermute(array, BOTH, across(major, mask))]
    pallas_call x0 -> x5, Pallas kernels: none -> 53.8 us  [the longest x3 27.3 us: project(): pl.pallas_call(kernel, in_specs=[SMEM] + [VMEM] * len(blocks) + [HBM], ou...]
    dot_general x6 -> x2, matrix products: 48.9 us -> 1.29 us  [the longest x1 1.05 us: attend_local(): jnp.einsum('shqk,skd->sqhd', probs, value_one, preferred_element_type=F32)]
    psum x1 -> x0, blocking collectives: 13.2 us -> none  [per_device(): squares = lax.psum(jnp.sum(wide * wide, axis=1), 'gy')]
    concatenate x1 -> x10, other arithmetic: 5.23 us -> 0.42 us  [the longest x3 0.2 us: per_device(): theirs = swap(jnp.concatenate(mine))]
  transfers between devices with their start and end apart: 6 -> 43, of which waited for: 6 -> 24; matrix products, arithmetic and copies ran while one was open for 0% -> 4% of each run, Pallas kernels for 0% -> 21%
where the time goes in v1:
time: 255 us
  waiting for transfers between devices  112 us (44%)
  starting transfers between devices  56.1 us (22%)
  Pallas kernels  53.8 us (21%)
  between operations  15.3 us (6%)
  other arithmetic  10.4 us (4%)
  local copies, waits for them, and re-layouts  5.86 us (2%)
    ppermute x27, waiting for transfers between devices, move(): return lax.ppermute(array, BOTH, across(major, mask))  62.3 us
    ppermute x27, starting transfers between devices, move(): return lax.ppermute(array, BOTH, across(major, mask))  39.7 us
    pallas_call x3, Pallas kernels, project(): pl.pallas_call(kernel, in_specs=[SMEM] + [VMEM] * len(blocks) + [HBM], ou...  27.3 us
    pallas_call x2, Pallas kernels, gate_and_up(): pl.pallas_call(kernel, in_specs=[SMEM] + [VMEM] * 4 + [HBM] * 2, out_spec...  26.6 us
    ppermute x3, waiting for transfers between devices, gather_x(): other = lax.ppermute(block, 'gy', across_x((1, 3)))  16.4 us
    ppermute x2, waiting for transfers between devices, sum_over_x(): arrived = lax.ppermute(sent, 'gy', across_x((3, 1)))  14.3 us
    ppermute x3, waiting for transfers between devices, gather_x(): lax.ppermute(jnp.concatenate([block, other]), 'gy', across_x((3, 1)))  9.58 us
    ppermute x3, starting transfers between devices, gather_x(): lax.ppermute(jnp.concatenate([block, other]), 'gy', across_x((3, 1)))  8.59 us
  transfers between devices with their start and end apart: 43, of which 24 were waited for; matrix products, arithmetic and copies ran while one was open for 4% of the time, Pallas kernels for 21%

profile of v1, /device:TPU:0, one launch (start us, length us, event | category | flops | bytes accessed | tf_op | source)
XLA Modules:
  0.0 254.7 jit_solution(10995057802608177497)
XLA Ops:
  12.7 4.8 %collective-permute-done.refs_1_ = bf16[128,1024]{1,0:T(8,128)(2,1)S(1)} collective-permute-done((bf16[128,1024]{1,0:T(8,128)(2,1)S(1)}, bf16[128,1024]{1,0:T(8,128)(2,1)S(1)}, u32[]{:S(2)}, u32[]{:S(2)}) %collective-permute-start) | collective-permute-done | bytes 262176 | tf_op jit(solution)/shard_map/ppermute | solution.py:86
  17.5 2.9 %collective-permute-start.1 = (bf16[256,1024]{1,0:T(8,128)(2,1)S(1)}, bf16[256,1024]{1,0:T(8,128)(2,1)S(1)}, u32[]{:S(2)}, u32[]{:S(2)}) collective-permute-start(bf16[256,1024]{1,0:T(8,128)(2,1)S(1)} %pad_maximum_fusion.5), channel_id=1, source_target_pairs={{0,6},{1,3},{2,4},{3,1},{4,2},{5,7},{6,0},{7,5},{8,14},{9,11},{10,... | collective-permute-start | bytes 1572872 | tf_op jit(solution)/shard_map/ppermute | solution.py:87
  20.4 7.6 %collective-permute-done.1.refs_2_ = bf16[256,1024]{1,0:T(8,128)(2,1)S(1)} collective-permute-done((bf16[256,1024]{1,0:T(8,128)(2,1)S(1)}, bf16[256,1024]{1,0:T(8,128)(2,1)S(1)}, u32[]{:S(2)}, u32[]{:S(2)}) %collective-permute-start.1) | collective-permute-done | bytes 524320 | tf_op jit(solution)/shard_map/ppermute | solution.py:87
  31.8 10.2 %shard_map.109 = (bf16[256,2048]{1,0:T(8,128)(2,1)}, bf16[256,2048]{1,0:T(8,128)(2,1)}, bf16[256,2048]{1,0:T(8,128)(2,1)}, bf16[256,2048]{1,0:T(8,128)(2,1)}) custom-call(s32[16]{0:T(128)S(1)} %select_n.94.places, bf16[128,1024]{1,0:T(8,128)(2,1)S(1)} %copy.44.refs_0_, bf16[128,1024]{1,0:T(8,128)(2,1)S(1)} %collective-permute-done.refs_1_, ...), custom_call_target="tpu_custom_call" | custom-call | flops 4294967296 | bytes 4194304 | tf_op jit(solution)/shard_map/pallas_call | solution.py:150
  42.0 4.0 %collective-permute-start.3 = (bf16[256,2048]{1,0:T(8,128)(2,1)}, bf16[256,2048]{1,0:T(8,128)(2,1)S(1)}, u32[]{:S(2)}, u32[]{:S(2)}) collective-permute-start(bf16[256,2048]{1,0:T(8,128)(2,1)} %get-tuple-element.26), channel_id=1, source_target_pairs={{0,16},{1,65},{2,18},{3,67},{4,20},{5,69},{6,22},{7,71},{8,24},{9,... | collective-permute-start | bytes 3145736 | tf_op jit(solution)/shard_map/ppermute | solution.py:77
  48.3 10.8 %collective-permute-done.3 = bf16[256,2048]{1,0:T(8,128)(2,1)S(1)} collective-permute-done((bf16[256,2048]{1,0:T(8,128)(2,1)}, bf16[256,2048]{1,0:T(8,128)(2,1)S(1)}, u32[]{:S(2)}, u32[]{:S(2)}) %collective-permute-start.3) | collective-permute-done | bytes 1048608 | tf_op jit(solution)/shard_map/ppermute | solution.py:77
  59.1 13.5 %collective-permute-done.4 = bf16[256,2048]{1,0:T(8,128)(2,1)S(1)} collective-permute-done((bf16[256,2048]{1,0:T(8,128)(2,1)}, bf16[256,2048]{1,0:T(8,128)(2,1)S(1)}, u32[]{:S(2)}, u32[]{:S(2)}) %collective-permute-start.4) | collective-permute-done | bytes 1048608 | tf_op jit(solution)/shard_map/ppermute | solution.py:77
  72.6 2.4 add_convert_fusion.5
  74.9 3.1 %collective-permute-start.6 = (bf16[64,2048]{1,0:T(8,128)(2,1)}, bf16[64,2048]{1,0:T(8,128)(2,1)S(1)}, u32[]{:S(2)}, u32[]{:S(2)}) collective-permute-start(bf16[64,2048]{1,0:T(8,128)(2,1)} %get-tuple-element.50), channel_id=1, source_target_pairs={{0,64},{1,17},{2,66},{3,19},{4,68},{5,21},{6,70},{7,23},{8,72},{9,... | collective-permute-start | bytes 786440 | tf_op jit(solution)/shard_map/ppermute | solution.py:77
  79.2 3.9 %collective-permute-done.6 = bf16[64,2048]{1,0:T(8,128)(2,1)S(1)} collective-permute-done((bf16[64,2048]{1,0:T(8,128)(2,1)}, bf16[64,2048]{1,0:T(8,128)(2,1)S(1)}, u32[]{:S(2)}, u32[]{:S(2)}) %collective-permute-start.6) | collective-permute-done | bytes 262176 | tf_op jit(solution)/shard_map/ppermute | solution.py:77
  83.0 3.0 %collective-permute-done.8 = bf16[64,2048]{1,0:T(8,128)(2,1)} collective-permute-done((bf16[64,2048]{1,0:T(8,128)(2,1)}, bf16[64,2048]{1,0:T(8,128)(2,1)}, u32[]{:S(2)}, u32[]{:S(2)}) %collective-permute-start.8) | collective-permute-done | bytes 262176 | tf_op jit(solution)/shard_map/ppermute | solution.py:77
  90.8 2.7 %collective-permute-start.12 = (bf16[32,4224]{1,0:T(8,128)(2,1)S(1)}, bf16[32,4224]{1,0:T(8,128)(2,1)S(1)}, u32[]{:S(2)}, u32[]{:S(2)}) collective-permute-start(bf16[32,4224]{1,0:T(8,128)(2,1)S(1)} %fusion.10), channel_id=1, source_target_pairs={{0,96},{1,25},{2,98},{3,27},{4,100},{5,29},{6,102},{7,31},{8,104},... | collective-permute-start | bytes 811016 | tf_op jit(solution)/shard_map/ppermute | solution.py:77
  95.1 5.3 %collective-permute-done.12 = bf16[32,4224]{1,0:T(8,128)(2,1)S(1)} collective-permute-done((bf16[32,4224]{1,0:T(8,128)(2,1)S(1)}, bf16[32,4224]{1,0:T(8,128)(2,1)S(1)}, u32[]{:S(2)}, u32[]{:S(2)}) %collective-permute-start.12) | collective-permute-done | bytes 270368 | tf_op jit(solution)/shard_map/ppermute | solution.py:77
  102.5 2.7 %collective-permute-start.15 = (bf16[64,4224]{1,0:T(8,128)(2,1)S(1)}, bf16[64,4224]{1,0:T(8,128)(2,1)S(1)}, u32[]{:S(2)}, u32[]{:S(2)}) collective-permute-start(bf16[64,4224]{1,0:T(8,128)(2,1)S(1)} %pad_maximum_fusion.3.refs_0_), channel_id=1, source_target_pairs={{0,24},{1,97},{2,26},{3,99},{4,28},{5,101},{6,30},{7,103},{8,16},{... | collective-permute-start | bytes 1622024 | tf_op jit(solution)/shard_map/ppermute | solution.py:77
  106.7 2.7 %collective-permute-start.29 = (bf16[64,4224]{1,0:T(8,128)(2,1)S(1)}, bf16[64,4224]{1,0:T(8,128)(2,1)}, u32[]{:S(2)}, u32[]{:S(2)}) collective-permute-start(bf16[64,4224]{1,0:T(8,128)(2,1)S(1)} %pad_maximum_fusion.4.refs_0_), channel_id=1, source_target_pairs={{0,24},{1,97},{2,26},{3,99},{4,28},{5,101},{6,30},{7,103},{8,16},{... | collective-permute-start | bytes 1622024 | tf_op jit(solution)/shard_map/ppermute | solution.py:77
  109.9 9.1 %collective-permute-done.15.refs_3_ = bf16[64,4224]{1,0:T(8,128)(2,1)S(1)} collective-permute-done((bf16[64,4224]{1,0:T(8,128)(2,1)S(1)}, bf16[64,4224]{1,0:T(8,128)(2,1)S(1)}, u32[]{:S(2)}, u32[]{:S(2)}) %collective-permute-start.15) | collective-permute-done | bytes 540704 | tf_op jit(solution)/shard_map/ppermute | solution.py:77
  119.9 13.3 %shard_map.110 = (bf16[128,3456]{1,0:T(8,128)(2,1)}, bf16[128,3456]{1,0:T(8,128)(2,1)}) custom-call(s32[4]{0:T(128)S(1)} %compare_select_fusion.2.places, bf16[64,4224]{1,0:T(8,128)(2,1)S(1)} %pad_maximum_fusion.3.refs_0_, bf16[64,4224]{1,0:T(8,128)(2,1)S(1)} %collective-permute-done.13.refs_1_, bf16[64,4224]{1,0:T(8,128)(2,1)S(1)} %collective-permute-done.14.refs_2_, ...), custom_call_target="tpu_custom_call" | custom-call | flops 6979321856 | bytes 27262976 | tf_op jit(solution)/shard_map/pallas_call | solution.py:239
  133.2 3.0 %collective-permute-start.16 = (bf16[128,3456]{1,0:T(8,128)(2,1)}, bf16[128,3456]{1,0:T(8,128)(2,1)}, u32[]{:S(2)}, u32[]{:S(2)}) collective-permute-start(bf16[128,3456]{1,0:T(8,128)(2,1)} %get-tuple-element.30), channel_id=1, source_target_pairs={{0,6},{1,3},{2,4},{3,1},{4,2},{5,7},{6,0},{7,5},{8,14},{9,11},{10,... | collective-permute-start | bytes 2654216 | tf_op jit(solution)/shard_map/ppermute | solution.py:258
  136.2 13.3 %shard_map.112 = (bf16[128,3456]{1,0:T(8,128)(2,1)}, bf16[128,3456]{1,0:T(8,128)(2,1)}) custom-call(s32[4]{0:T(128)S(1)} %compare_select_fusion.2.places, bf16[64,4224]{1,0:T(8,128)(2,1)S(1)} %pad_maximum_fusion.4.refs_0_, bf16[64,4224]{1,0:T(8,128)(2,1)S(1)} %collective-permute-done.27.refs_1_, bf16[64,4224]{1,0:T(8,128)(2,1)S(1)} %collective-permute-done.28.refs_2_, ...), custom_call_target="tpu_custom_call" | custom-call | flops 6979321856 | bytes 27262976 | tf_op jit(solution)/shard_map/pallas_call | solution.py:239
  151.3 14.3 %collective-permute-done.30 = bf16[128,3456]{1,0:T(8,128)(2,1)S(1)} collective-permute-done((bf16[128,3456]{1,0:T(8,128)(2,1)}, bf16[128,3456]{1,0:T(8,128)(2,1)S(1)}, u32[]{:S(2)}, u32[]{:S(2)}) %collective-permute-start.30) | collective-permute-done | bytes 884768 | tf_op jit(solution)/shard_map/ppermute | solution.py:258
  170.5 5.9 %collective-permute-done.18.refs_1_ = bf16[64,1664]{1,0:T(8,128)(2,1)S(1)} collective-permute-done((bf16[64,1664]{1,0:T(8,128)(2,1)S(1)}, bf16[64,1664]{1,0:T(8,128)(2,1)S(1)}, u32[]{:S(2)}, u32[]{:S(2)}) %collective-permute-start.18) | collective-permute-done | bytes 213024 | tf_op jit(solution)/shard_map/ppermute | solution.py:86
  176.4 2.8 %collective-permute-start.19 = (bf16[128,1664]{1,0:T(8,128)(2,1)S(1)}, bf16[128,1664]{1,0:T(8,128)(2,1)S(1)}, u32[]{:S(2)}, u32[]{:S(2)}) collective-permute-start(bf16[128,1664]{1,0:T(8,128)(2,1)S(1)} %pad_maximum_fusion.6), channel_id=1, source_target_pairs={{0,6},{1,3},{2,4},{3,1},{4,2},{5,7},{6,0},{7,5},{8,14},{9,11},{10,... | collective-permute-start | bytes 1277960 | tf_op jit(solution)/shard_map/ppermute | solution.py:87
  179.3 4.3 %collective-permute-done.31 = bf16[64,3456]{1,0:T(8,128)(2,1)S(1)} collective-permute-done((bf16[64,3456]{1,0:T(8,128)(2,1)S(1)}, bf16[64,3456]{1,0:T(8,128)(2,1)S(1)}, u32[]{:S(2)}, u32[]{:S(2)}) %collective-permute-start.31) | collective-permute-done | bytes 442400 | tf_op jit(solution)/shard_map/ppermute | solution.py:262
  186.4 5.8 %collective-permute-done.32.refs_1_ = bf16[64,1664]{1,0:T(8,128)(2,1)S(1)} collective-permute-done((bf16[64,1664]{1,0:T(8,128)(2,1)S(1)}, bf16[64,1664]{1,0:T(8,128)(2,1)S(1)}, u32[]{:S(2)}, u32[]{:S(2)}) %collective-permute-start.32) | collective-permute-done | bytes 213024 | tf_op jit(solution)/shard_map/ppermute | solution.py:86
  192.2 2.8 %collective-permute-start.33 = (bf16[128,1664]{1,0:T(8,128)(2,1)S(1)}, bf16[128,1664]{1,0:T(8,128)(2,1)S(1)}, u32[]{:S(2)}, u32[]{:S(2)}) collective-permute-start(bf16[128,1664]{1,0:T(8,128)(2,1)S(1)} %pad_maximum_fusion.7), channel_id=1, source_target_pairs={{0,6},{1,3},{2,4},{3,1},{4,2},{5,7},{6,0},{7,5},{8,14},{9,11},{10,... | collective-permute-start | bytes 1277960 | tf_op jit(solution)/shard_map/ppermute | solution.py:87
  195.1 8.6 %shard_map.111 = (bf16[128,2048]{1,0:T(8,128)(2,1)S(1)}, bf16[128,2048]{1,0:T(8,128)(2,1)S(1)}, bf16[128,2048]{1,0:T(8,128)(2,1)}, bf16[128,2048]{1,0:T(8,128)(2,1)}) custom-call(s32[32]{0:T(128)S(1)} %reshape.426.places, bf16[64,1664]{1,0:T(8,128)(2,1)S(1)} %fusion.8.refs_0_, bf16[64,1664]{1,0:T(8,128)(2,1)S(1)} %collective-permute-done.18.refs_1_, ...), custom_call_target="tpu_custom_call" | custom-call | flops 3489660928 | bytes 6815744 | tf_op jit(solution)/shard_map/pallas_call | solution.py:150
  204.7 2.4 collective-permute-start.21
  209.7 8.5 %shard_map.113 = (bf16[128,2048]{1,0:T(8,128)(2,1)S(1)}, bf16[128,2048]{1,0:T(8,128)(2,1)S(1)}, bf16[128,2048]{1,0:T(8,128)(2,1)}, bf16[128,2048]{1,0:T(8,128)(2,1)}) custom-call(s32[32]{0:T(128)S(1)} %reshape.426.places, bf16[64,1664]{1,0:T(8,128)(2,1)S(1)} %fusion.6.refs_0_, bf16[64,1664]{1,0:T(8,128)(2,1)S(1)} %collective-permute-done.32.refs_1_, ...), custom_call_target="tpu_custom_call" | custom-call | flops 3489660928 | bytes 6815744 | tf_op jit(solution)/shard_map/pallas_call | solution.py:150
  218.3 2.5 collective-permute-start.35
  226.8 4.0 %collective-permute-done.35 = bf16[128,2048]{1,0:T(8,128)(2,1)S(1)} collective-permute-done((bf16[128,2048]{1,0:T(8,128)(2,1)}, bf16[128,2048]{1,0:T(8,128)(2,1)S(1)}, u32[]{:S(2)}, u32[]{:S(2)}) %collective-permute-start.35) | collective-permute-done | bytes 524320 | tf_op jit(solution)/shard_map/ppermute | solution.py:77
  232.1 5.6 %collective-permute-done.36 = bf16[128,2048]{1,0:T(8,128)(2,1)S(1)} collective-permute-done((bf16[128,2048]{1,0:T(8,128)(2,1)S(1)}, bf16[128,2048]{1,0:T(8,128)(2,1)S(1)}, u32[]{:S(2)}, u32[]{:S(2)}) %collective-permute-start.36) | collective-permute-done | bytes 524320 | tf_op jit(solution)/shard_map/ppermute | solution.py:77
  242.2 2.3 collective-permute-done.38
  (152 shorter events, 51.5 us)
Async XLA Ops:
  6.5 113.3 %all-gather.3.cloned.1.call-start = ((), (), s32[]{:S(2)}) async-start(), calls=%async_computation | async-start | bytes 20447232 | tf_op jit(solution)/shard_map/all_gather | solution.py:280
  7.3 112.6 %all-gather.5.cloned.1.call-start = ((), (), s32[]{:S(2)}) async-start(), calls=%async_computation.1 | async-start | bytes 20447232 | tf_op jit(solution)/shard_map/all_gather | solution.py:281
  17.5 10.5 %collective-permute-start.1 = (bf16[256,1024]{1,0:T(8,128)(2,1)S(1)}, bf16[256,1024]{1,0:T(8,128)(2,1)S(1)}, u32[]{:S(2)}, u32[]{:S(2)}) collective-permute-start(bf16[256,1024]{1,0:T(8,128)(2,1)S(1)} %pad_maximum_fusion.5), channel_id=1, source_target_pairs={{0,6},{1,3},{2,4},{3,1},{4,2},{5,7},{6,0},{7,5},{8,14},{9,11},{10,... | collective-permute-start | bytes 1572872 | tf_op jit(solution)/shard_map/ppermute | solution.py:87
  42.0 17.1 %collective-permute-start.3 = (bf16[256,2048]{1,0:T(8,128)(2,1)}, bf16[256,2048]{1,0:T(8,128)(2,1)S(1)}, u32[]{:S(2)}, u32[]{:S(2)}) collective-permute-start(bf16[256,2048]{1,0:T(8,128)(2,1)} %get-tuple-element.26), channel_id=1, source_target_pairs={{0,16},{1,65},{2,18},{3,67},{4,20},{5,69},{6,22},{7,71},{8,24},{9,... | collective-permute-start | bytes 3145736 | tf_op jit(solution)/shard_map/ppermute | solution.py:77
  46.0 26.6 %collective-permute-start.4 = (bf16[256,2048]{1,0:T(8,128)(2,1)}, bf16[256,2048]{1,0:T(8,128)(2,1)S(1)}, u32[]{:S(2)}, u32[]{:S(2)}) collective-permute-start(bf16[256,2048]{1,0:T(8,128)(2,1)} %get-tuple-element.27), channel_id=1, source_target_pairs={{0,8},{1,33},{2,10},{3,35},{4,12},{5,37},{6,14},{7,39},{8,0},{9,41... | collective-permute-start | bytes 3145736 | tf_op jit(solution)/shard_map/ppermute | solution.py:77
  48.3 24.3 %collective-permute-start.5 = (bf16[256,2048]{1,0:T(8,128)(2,1)}, bf16[256,2048]{1,0:T(8,128)(2,1)S(1)}, u32[]{:S(2)}, u32[]{:S(2)}) collective-permute-start(bf16[256,2048]{1,0:T(8,128)(2,1)} %get-tuple-element.28), channel_id=1, source_target_pairs={{0,24},{1,97},{2,26},{3,99},{4,28},{5,101},{6,30},{7,103},{8,16},{... | collective-permute-start | bytes 3145736 | tf_op jit(solution)/shard_map/ppermute | solution.py:77
  74.9 8.1 %collective-permute-start.6 = (bf16[64,2048]{1,0:T(8,128)(2,1)}, bf16[64,2048]{1,0:T(8,128)(2,1)S(1)}, u32[]{:S(2)}, u32[]{:S(2)}) collective-permute-start(bf16[64,2048]{1,0:T(8,128)(2,1)} %get-tuple-element.50), channel_id=1, source_target_pairs={{0,64},{1,17},{2,66},{3,19},{4,68},{5,21},{6,70},{7,23},{8,72},{9,... | collective-permute-start | bytes 786440 | tf_op jit(solution)/shard_map/ppermute | solution.py:77
  90.8 9.6 %collective-permute-start.12 = (bf16[32,4224]{1,0:T(8,128)(2,1)S(1)}, bf16[32,4224]{1,0:T(8,128)(2,1)S(1)}, u32[]{:S(2)}, u32[]{:S(2)}) collective-permute-start(bf16[32,4224]{1,0:T(8,128)(2,1)S(1)} %fusion.10), channel_id=1, source_target_pairs={{0,96},{1,25},{2,98},{3,27},{4,100},{5,29},{6,102},{7,31},{8,104},... | collective-permute-start | bytes 811016 | tf_op jit(solution)/shard_map/ppermute | solution.py:77
  94.4 8.1 %collective-permute-start.10 = (bf16[32,4224]{1,0:T(8,128)(2,1)S(1)}, bf16[32,4224]{1,0:T(8,128)(2,1)S(1)}, u32[]{:S(2)}, u32[]{:S(2)}) collective-permute-start(bf16[32,4224]{1,0:T(8,128)(2,1)S(1)} %fusion.10), channel_id=1, source_target_pairs={{0,32},{1,9},{2,34},{3,11},{4,36},{5,13},{6,38},{7,15},{8,40},{9,1... | collective-permute-start | bytes 811016 | tf_op jit(solution)/shard_map/ppermute | solution.py:77
  102.5 16.4 %collective-permute-start.15 = (bf16[64,4224]{1,0:T(8,128)(2,1)S(1)}, bf16[64,4224]{1,0:T(8,128)(2,1)S(1)}, u32[]{:S(2)}, u32[]{:S(2)}) collective-permute-start(bf16[64,4224]{1,0:T(8,128)(2,1)S(1)} %pad_maximum_fusion.3.refs_0_), channel_id=1, source_target_pairs={{0,24},{1,97},{2,26},{3,99},{4,28},{5,101},{6,30},{7,103},{8,16},{... | collective-permute-start | bytes 1622024 | tf_op jit(solution)/shard_map/ppermute | solution.py:77
  105.2 13.7 %collective-permute-start.14 = (bf16[64,4224]{1,0:T(8,128)(2,1)S(1)}, bf16[64,4224]{1,0:T(8,128)(2,1)S(1)}, u32[]{:S(2)}, u32[]{:S(2)}) collective-permute-start(bf16[64,4224]{1,0:T(8,128)(2,1)S(1)} %pad_maximum_fusion.3.refs_0_), channel_id=1, source_target_pairs={{0,16},{1,65},{2,18},{3,67},{4,20},{5,69},{6,22},{7,71},{8,24},{9,... | collective-permute-start | bytes 1622024 | tf_op jit(solution)/shard_map/ppermute | solution.py:77
  105.7 14.2 %collective-permute-start.13 = (bf16[64,4224]{1,0:T(8,128)(2,1)S(1)}, bf16[64,4224]{1,0:T(8,128)(2,1)S(1)}, u32[]{:S(2)}, u32[]{:S(2)}) collective-permute-start(bf16[64,4224]{1,0:T(8,128)(2,1)S(1)} %pad_maximum_fusion.3.refs_0_), channel_id=1, source_target_pairs={{0,8},{1,33},{2,10},{3,35},{4,12},{5,37},{6,14},{7,39},{8,0},{9,41... | collective-permute-start | bytes 1622024 | tf_op jit(solution)/shard_map/ppermute | solution.py:77
  106.7 29.5 %collective-permute-start.29 = (bf16[64,4224]{1,0:T(8,128)(2,1)S(1)}, bf16[64,4224]{1,0:T(8,128)(2,1)}, u32[]{:S(2)}, u32[]{:S(2)}) collective-permute-start(bf16[64,4224]{1,0:T(8,128)(2,1)S(1)} %pad_maximum_fusion.4.refs_0_), channel_id=1, source_target_pairs={{0,24},{1,97},{2,26},{3,99},{4,28},{5,101},{6,30},{7,103},{8,16},{... | collective-permute-start | bytes 1622024 | tf_op jit(solution)/shard_map/ppermute | solution.py:77
  109.4 26.8 %collective-permute-start.28 = (bf16[64,4224]{1,0:T(8,128)(2,1)S(1)}, bf16[64,4224]{1,0:T(8,128)(2,1)S(1)}, u32[]{:S(2)}, u32[]{:S(2)}) collective-permute-start(bf16[64,4224]{1,0:T(8,128)(2,1)S(1)} %pad_maximum_fusion.4.refs_0_), channel_id=1, source_target_pairs={{0,16},{1,65},{2,18},{3,67},{4,20},{5,69},{6,22},{7,71},{8,24},{9,... | collective-permute-start | bytes 1622024 | tf_op jit(solution)/shard_map/ppermute | solution.py:77
  119.0 17.3 %collective-permute-start.27 = (bf16[64,4224]{1,0:T(8,128)(2,1)S(1)}, bf16[64,4224]{1,0:T(8,128)(2,1)S(1)}, u32[]{:S(2)}, u32[]{:S(2)}) collective-permute-start(bf16[64,4224]{1,0:T(8,128)(2,1)S(1)} %pad_maximum_fusion.4.refs_0_), channel_id=1, source_target_pairs={{0,8},{1,33},{2,10},{3,35},{4,12},{5,37},{6,14},{7,39},{8,0},{9,41... | collective-permute-start | bytes 1622024 | tf_op jit(solution)/shard_map/ppermute | solution.py:77
  133.2 16.9 %collective-permute-start.16 = (bf16[128,3456]{1,0:T(8,128)(2,1)}, bf16[128,3456]{1,0:T(8,128)(2,1)}, u32[]{:S(2)}, u32[]{:S(2)}) collective-permute-start(bf16[128,3456]{1,0:T(8,128)(2,1)} %get-tuple-element.30), channel_id=1, source_target_pairs={{0,6},{1,3},{2,4},{3,1},{4,2},{5,7},{6,0},{7,5},{8,14},{9,11},{10,... | collective-permute-start | bytes 2654216 | tf_op jit(solution)/shard_map/ppermute | solution.py:258
  149.5 16.1 %collective-permute-start.30 = (bf16[128,3456]{1,0:T(8,128)(2,1)}, bf16[128,3456]{1,0:T(8,128)(2,1)S(1)}, u32[]{:S(2)}, u32[]{:S(2)}) collective-permute-start(bf16[128,3456]{1,0:T(8,128)(2,1)} %get-tuple-element.36), channel_id=1, source_target_pairs={{0,6},{1,3},{2,4},{3,1},{4,2},{5,7},{6,0},{7,5},{8,14},{9,11},{10,... | collective-permute-start | bytes 2654216 | tf_op jit(solution)/shard_map/ppermute | solution.py:258
  151.2 15.5 %collective-permute-start.17 = (bf16[64,3456]{1,0:T(8,128)(2,1)S(1)}, bf16[64,3456]{1,0:T(8,128)(2,1)S(1)}, u32[]{:S(2)}, u32[]{:S(2)}) collective-permute-start(bf16[64,3456]{1,0:T(8,128)(2,1)S(1)} %add_convert_fusion.1), channel_id=1, source_target_pairs={{0,2},{1,7},{2,0},{3,5},{4,6},{5,3},{6,4},{7,1},{8,10},{9,15},{10,... | collective-permute-start | bytes 1327112 | tf_op jit(solution)/shard_map/ppermute | solution.py:262
  168.3 8.1 %collective-permute-start.18 = (bf16[64,1664]{1,0:T(8,128)(2,1)S(1)}, bf16[64,1664]{1,0:T(8,128)(2,1)S(1)}, u32[]{:S(2)}, u32[]{:S(2)}) collective-permute-start(bf16[64,1664]{1,0:T(8,128)(2,1)S(1)} %fusion.8.refs_0_), channel_id=1, source_target_pairs={{0,2},{1,7},{2,0},{3,5},{4,6},{5,3},{6,4},{7,1},{8,10},{9,15},{10,... | collective-permute-start | bytes 638984 | tf_op jit(solution)/shard_map/ppermute | solution.py:86
  168.4 15.1 %collective-permute-start.31 = (bf16[64,3456]{1,0:T(8,128)(2,1)S(1)}, bf16[64,3456]{1,0:T(8,128)(2,1)S(1)}, u32[]{:S(2)}, u32[]{:S(2)}) collective-permute-start(bf16[64,3456]{1,0:T(8,128)(2,1)S(1)} %add_convert_fusion), channel_id=1, source_target_pairs={{0,2},{1,7},{2,0},{3,5},{4,6},{5,3},{6,4},{7,1},{8,10},{9,15},{10,... | collective-permute-start | bytes 1327112 | tf_op jit(solution)/shard_map/ppermute | solution.py:262
  176.4 9.4 %collective-permute-start.19 = (bf16[128,1664]{1,0:T(8,128)(2,1)S(1)}, bf16[128,1664]{1,0:T(8,128)(2,1)S(1)}, u32[]{:S(2)}, u32[]{:S(2)}) collective-permute-start(bf16[128,1664]{1,0:T(8,128)(2,1)S(1)} %pad_maximum_fusion.6), channel_id=1, source_target_pairs={{0,6},{1,3},{2,4},{3,1},{4,2},{5,7},{6,0},{7,5},{8,14},{9,11},{10,... | collective-permute-start | bytes 1277960 | tf_op jit(solution)/shard_map/ppermute | solution.py:87
  185.9 9.2 %collective-permute-start.20 = (bf16[256,1664]{1,0:T(8,128)(2,1)S(1)}, bf16[256,1664]{1,0:T(8,128)(2,1)}, u32[]{:S(2)}, u32[]{:S(2)}) collective-permute-start(bf16[256,1664]{1,0:T(8,128)(2,1)S(1)} %pad_maximum_fusion.1), channel_id=1, source_target_pairs={{0,1},{1,0},{2,3},{3,2},{4,5},{5,4},{6,7},{7,6},{8,9},{9,8},{10,11... | collective-permute-start | bytes 2555912 | tf_op jit(solution)/shard_map/ppermute | solution.py:95
  192.2 11.5 %collective-permute-start.33 = (bf16[128,1664]{1,0:T(8,128)(2,1)S(1)}, bf16[128,1664]{1,0:T(8,128)(2,1)S(1)}, u32[]{:S(2)}, u32[]{:S(2)}) collective-permute-start(bf16[128,1664]{1,0:T(8,128)(2,1)S(1)} %pad_maximum_fusion.7), channel_id=1, source_target_pairs={{0,6},{1,3},{2,4},{3,1},{4,2},{5,7},{6,0},{7,5},{8,14},{9,11},{10,... | collective-permute-start | bytes 1277960 | tf_op jit(solution)/shard_map/ppermute | solution.py:87
  204.7 17.2 %collective-permute-start.21 = (bf16[128,2048]{1,0:T(8,128)(2,1)S(1)}, bf16[128,2048]{1,0:T(8,128)(2,1)S(1)}, u32[]{:S(2)}, u32[]{:S(2)}) collective-permute-start(bf16[128,2048]{1,0:T(8,128)(2,1)S(1)} %copy-done.13), channel_id=1, source_target_pairs={{0,16},{1,65},{2,18},{3,67},{4,20},{5,69},{6,22},{7,71},{8,24},{9,... | collective-permute-start | bytes 1572872 | tf_op jit(solution)/shard_map/ppermute | solution.py:77
  207.1 15.4 %collective-permute-start.22 = (bf16[128,2048]{1,0:T(8,128)(2,1)S(1)}, bf16[128,2048]{1,0:T(8,128)(2,1)S(1)}, u32[]{:S(2)}, u32[]{:S(2)}) collective-permute-start(bf16[128,2048]{1,0:T(8,128)(2,1)S(1)} %get-tuple-element.33), channel_id=1, source_target_pairs={{0,8},{1,33},{2,10},{3,35},{4,12},{5,37},{6,14},{7,39},{8,0},{9,41... | collective-permute-start | bytes 1572872 | tf_op jit(solution)/shard_map/ppermute | solution.py:77
  208.2 14.3 %collective-permute-start.23 = (bf16[128,2048]{1,0:T(8,128)(2,1)S(1)}, bf16[128,2048]{1,0:T(8,128)(2,1)S(1)}, u32[]{:S(2)}, u32[]{:S(2)}) collective-permute-start(bf16[128,2048]{1,0:T(8,128)(2,1)S(1)} %copy-done.12), channel_id=1, source_target_pairs={{0,24},{1,97},{2,26},{3,99},{4,28},{5,101},{6,30},{7,103},{8,16},{... | collective-permute-start | bytes 1572872 | tf_op jit(solution)/shard_map/ppermute | solution.py:77
  218.3 12.5 %collective-permute-start.35 = (bf16[128,2048]{1,0:T(8,128)(2,1)}, bf16[128,2048]{1,0:T(8,128)(2,1)S(1)}, u32[]{:S(2)}, u32[]{:S(2)}) collective-permute-start(bf16[128,2048]{1,0:T(8,128)(2,1)} %get-tuple-element.42), channel_id=1, source_target_pairs={{0,16},{1,65},{2,18},{3,67},{4,20},{5,69},{6,22},{7,71},{8,24},{9,... | collective-permute-start | bytes 1572872 | tf_op jit(solution)/shard_map/ppermute | solution.py:77
  220.8 16.9 %collective-permute-start.36 = (bf16[128,2048]{1,0:T(8,128)(2,1)S(1)}, bf16[128,2048]{1,0:T(8,128)(2,1)S(1)}, u32[]{:S(2)}, u32[]{:S(2)}) collective-permute-start(bf16[128,2048]{1,0:T(8,128)(2,1)S(1)} %get-tuple-element.43), channel_id=1, source_target_pairs={{0,8},{1,33},{2,10},{3,35},{4,12},{5,37},{6,14},{7,39},{8,0},{9,41... | collective-permute-start | bytes 1572872 | tf_op jit(solution)/shard_map/ppermute | solution.py:77
  221.9 15.8 %collective-permute-start.37 = (bf16[128,2048]{1,0:T(8,128)(2,1)}, bf16[128,2048]{1,0:T(8,128)(2,1)S(1)}, u32[]{:S(2)}, u32[]{:S(2)}) collective-permute-start(bf16[128,2048]{1,0:T(8,128)(2,1)} %get-tuple-element.44), channel_id=1, source_target_pairs={{0,24},{1,97},{2,26},{3,99},{4,28},{5,101},{6,30},{7,103},{8,16},{... | collective-permute-start | bytes 1572872 | tf_op jit(solution)/shard_map/ppermute | solution.py:77
  222.8 19.2 %collective-permute-start.24 = (bf16[32,2048]{1,0:T(8,128)(2,1)S(1)}, bf16[32,2048]{1,0:T(8,128)(2,1)S(1)}, u32[]{:S(2)}, u32[]{:S(2)}) collective-permute-start(bf16[32,2048]{1,0:T(8,128)(2,1)S(1)} %get-tuple-element.53), channel_id=1, source_target_pairs={{0,64},{1,17},{2,66},{3,19},{4,68},{5,21},{6,70},{7,23},{8,72},{9,... | collective-permute-start | bytes 393224 | tf_op jit(solution)/shard_map/ppermute | solution.py:77
  225.0 17.0 %collective-permute-start.26 = (bf16[32,2048]{1,0:T(8,128)(2,1)S(1)}, bf16[32,2048]{1,0:T(8,128)(2,1)S(1)}, u32[]{:S(2)}, u32[]{:S(2)}) collective-permute-start(bf16[32,2048]{1,0:T(8,128)(2,1)S(1)} %get-tuple-element.54), channel_id=1, source_target_pairs={{0,96},{1,25},{2,98},{3,27},{4,100},{5,29},{6,102},{7,31},{8,104},... | collective-permute-start | bytes 393224 | tf_op jit(solution)/shard_map/ppermute | solution.py:77
  230.8 11.2 %collective-permute-start.25 = (bf16[32,2048]{1,0:T(8,128)(2,1)S(1)}, bf16[32,2048]{1,0:T(8,128)(2,1)S(1)}, u32[]{:S(2)}, u32[]{:S(2)}) collective-permute-start(bf16[32,2048]{1,0:T(8,128)(2,1)S(1)} %get-tuple-element.55), channel_id=1, source_target_pairs={{0,32},{1,9},{2,34},{3,11},{4,36},{5,13},{6,38},{7,15},{8,40},{9,1... | collective-permute-start | bytes 393224 | tf_op jit(solution)/shard_map/ppermute | solution.py:77
  (25 other events, 141.4 us)
Sparse Core Ops, SparseCore 0:
  9.0 31.6 all-gather.2
  42.4 30.5 all-gather.4

commit v2 on v1

--- a/solution.py
+++ b/solution.py
@@ -13,6 +13,8 @@
 SIDE = 4
 TILE = 256
 AHEAD = 6
+PIECES = 8
+PROJECT_BYTES = 12 * 1024 * 1024
 VMEM_BYTES = 52 * 1024 * 1024
 BF16 = jnp.bfloat16
 F32 = jnp.float32
@@ -82,8 +84,10 @@
     return [add_up([block[q * size : (q + 1) * size] for block in blocks]) for q in range(SIDE)]
 
 
-def gather_x(block):
+def gather_x(block, earlier=None):
     other = lax.ppermute(block, "gy", across_x((1, 3)))
+    if earlier is not None:
+        other = after(other, earlier)
     return [block, other, lax.ppermute(jnp.concatenate([block, other]), "gy", across_x((3, 1)))]
 
 
@@ -122,42 +126,60 @@
             i += 1
 
 
+def start_all(sources, targets, sems):
+    copies = []
+    for source, target in zip(sources, targets):
+        piece = source.shape[0] // PIECES
+        for j in range(PIECES):
+            at = pl.ds(j * piece, piece)
+            copies.append(
+                pltpu.make_async_copy(source.at[at], target.at[at], sems.at[len(copies)])
+            )
+    for copy in copies:
+        copy.start()
+    return copies
+
+
+def load(*weights):
+    count = len(weights)
+
+    def kernel(*refs):
+        for copy in start_all(refs[:count], refs[count : 2 * count], refs[-1]):
+            copy.wait()
+
+    return pl.pallas_call(
+        kernel,
+        in_specs=[HBM] * count,
+        out_specs=[VMEM] * count,
+        scratch_shapes=[pltpu.SemaphoreType.DMA((count * PIECES,))],
+        out_shape=[jax.ShapeDtypeStruct(weight.shape, BF16) for weight in weights],
+        compiler_params=pltpu.CompilerParams(vmem_limit_bytes=PROJECT_BYTES),
+        cost_estimate=pl.CostEstimate(
+            flops=0, bytes_accessed=sum(2 * weight.size for weight in weights), transcendentals=0
+        ),
+    )(*weights)
+
+
 def project(places, size, blocks, weight):
     depth, width = weight.shape
     rows = size * places.shape[0]
-    tiles = width // TILE
 
     def kernel(places, *refs):
-        given, weight_ref, outs = refs[: len(blocks)], refs[-8], refs[-7:-3]
-        lhs, tile_refs, sems = refs[-3:]
-
-        def copy(j):
-            at = pl.ds(pl.multiple_of(j * TILE, TILE), TILE)
-            return pltpu.make_async_copy(weight_ref.at[:, at], tile_refs.at[j], sems.at[j])
-
-        for j in range(tiles):
-            copy(j).start()
+        given, weight_ref, outs, lhs = refs[: len(blocks)], refs[-6], refs[-5:-1], refs[-1]
         fill(places, given, lhs, size)
-
-        @pl.loop(0, tiles)
-        def _(j):
-            copy(j).wait()
-            product = jnp.dot(lhs[...], tile_refs[j], preferred_element_type=F32).astype(BF16)
-            at = pl.ds(pl.multiple_of(j * TILE, TILE), TILE)
+        for first in range(0, width, TILE):
+            at = pl.ds(first, TILE)
+            product = jnp.dot(lhs[...], weight_ref[:, at], preferred_element_type=F32).astype(BF16)
             for e in range(4):
                 outs[e][:, at] = product[e * rows // 4 : (e + 1) * rows // 4]
 
     return pl.pallas_call(
         kernel,
-        in_specs=[SMEM] + [VMEM] * len(blocks) + [HBM],
+        in_specs=[SMEM] + [VMEM] * (len(blocks) + 1),
         out_specs=[VMEM] * 4,
-        scratch_shapes=[
-            pltpu.VMEM((rows, depth), BF16),
-            pltpu.VMEM((tiles, depth, TILE), BF16),
-            pltpu.SemaphoreType.DMA((tiles,)),
-        ],
+        scratch_shapes=[pltpu.VMEM((rows, depth), BF16)],
         out_shape=[jax.ShapeDtypeStruct((rows // 4, width), BF16)] * 4,
-        compiler_params=pltpu.CompilerParams(vmem_limit_bytes=VMEM_BYTES),
+        compiler_params=pltpu.CompilerParams(vmem_limit_bytes=PROJECT_BYTES),
         cost_estimate=pl.CostEstimate(
             flops=2 * rows * depth * width, bytes_accessed=2 * depth * width, transcendentals=0
         ),
@@ -255,10 +277,8 @@
 
 def sum_over_x(sent, kept, earlier):
     rows = sent.shape[0] // 2
-    arrived = lax.ppermute(sent, "gy", across_x((3, 1)))
+    arrived = after(lax.ppermute(sent, "gy", across_x((3, 1))), earlier)
     other = (kept[rows:].astype(F32) + arrived[rows:].astype(F32)).astype(BF16)
-    if earlier is not None:
-        other = after(other, earlier)
     other = lax.ppermute(other, "gy", across_x((1, 3)))
     return add_up([kept[:rows], arrived[:rows], other])
 
@@ -281,7 +301,8 @@
     w_up = lax.all_gather(w_up, "gy", axis=0, tiled=True, axis_index_groups=CORES)
 
     mine = attend_local(queries, keys, values, lengths, offsets)
-    mine = gather_x(mine)
+    (out_weight,) = load(after(w_out, mine))
+    mine = gather_x(mine, out_weight)
     theirs = swap(jnp.concatenate(mine))
     near = jnp.where(core == 0, 1, 3)
     zero, far = jnp.zeros_like(near), jnp.full_like(near, 2)
@@ -294,7 +315,7 @@
     in_y = (lines ^ y)[:, :, None]
     in_z = ((2 * cores[:, None] + two[None, :]) ^ z)[:, None, :]
     places = jnp.where(core == 0, 4 * in_z + in_y, 4 * in_y + in_z).reshape(16)
-    parts = sum_major(project(places, rows, mine + [theirs], w_out), rows)
+    parts = sum_major(project(places, rows, mine + [theirs], out_weight), rows)
     arrived = [move(parts[q].astype(BF16), False, q) for q in (2, 1, 3)]
     attn_proj = add_up([parts[0]] + arrived)
     wide = (resid_in.astype(F32) + attn_proj).astype(BF16).astype(F32)
@@ -310,26 +331,32 @@
     scaled = [scaled] + [move(scaled, False, q) for q in (1, 2, 3)]
 
     quarter = half // 2
-    outs, hidden = [], None
+    slot = x ^ here ^ four
+    slots = jnp.where(slot == 4 - near, 0, jnp.where(slot == 2, 1, jnp.where(slot == 0, 2, 3)))
+    products = []
     for chunk in range(2):
         taken = slice(chunk * quarter, (chunk + 1) * quarter)
         block = jnp.concatenate([block[taken] for block in scaled])
         blocks = [block] + [move(block, True, e) for e in (1, 2, 3)]
-        slot = x ^ here ^ four
-        slots = jnp.where(slot == 4 - near, 0, jnp.where(slot == 2, 1, jnp.where(slot == 0, 2, 3)))
-        both = sum_over_x(*gate_and_up(slots, blocks, w_gate, w_up), hidden)
+        products.append(gate_and_up(slots, blocks, w_gate, w_up))
+    outs, placed = [], None
+    for chunk, (sent, kept) in enumerate(products):
+        both = sum_over_x(sent, kept, hidden if chunk else products[1][0])
+        if not chunk:
+            (down_weight,) = load(after(w_down, products[1][0]))
+            both = after(both, down_weight)
         scale = lax.rsqrt(jnp.sum(both[:, 2 * units :], axis=1, keepdims=True) / D + 1e-05)
         gate, up = both[:, :units] * scale, both[:, units : 2 * units] * scale
         hidden = (jax.nn.silu(gate) * up).astype(BF16)
         mine = gather_x(hidden)
         if chunk:
-            mine = after(mine, *products)
+            mine = after(mine, *placed)
         theirs = swap(jnp.concatenate(mine))
         ours = 4 * (lines[0] ^ here)[:, None] + four[None, :]
         others = (lines[1] ^ there)[:, None] + 4 * four[None, :]
         places = jnp.stack([2 * ours + core, 2 * others + 1 - core]).reshape(32)
-        products = project(places, quarter, mine + [theirs], w_down)
-        parts = sum_major(products, half)
+        placed = project(places, quarter, mine + [theirs], down_weight)
+        parts = sum_major(placed, half)
         arrived = [move(parts[q].astype(BF16), False, q) for q in (2, 1, 3)]
         own = wide.reshape(2, 2, quarter, columns)[:, chunk].reshape(half, columns)
         outs.append((own + add_up([parts[0]] + arrived)).astype(BF16).reshape(2, quarter, columns))

time: 255 us -> 247 us (0.969)
  local copies, waits for them, and re-layouts: 5.86 us -> 20.4 us
  Pallas kernels: 53.8 us -> 42.5 us
  starting transfers between devices: 56.1 us -> 49.8 us
  other arithmetic: 10.4 us -> 7.03 us
    unnamed x28 -> x38, local copies, waits for them, and re-layouts: 4.46 us -> 19 us
    pallas_call x3 -> x5, Pallas kernels: 27.3 us -> 15.9 us  [the longest x3 14.4 us: project(): pl.pallas_call(kernel, in_specs=[SMEM] + [VMEM] * (len(blocks) + 1), out_...]
    ppermute x2, waiting for transfers between devices: 14.3 us -> 3.15 us  [sum_over_x(): arrived = after(lax.ppermute(sent, 'gy', across_x((3, 1))), earlier)]
    ppermute x2, waiting for transfers between devices: 4.29 us -> 12.3 us  [sum_over_x(): other = lax.ppermute(other, 'gy', across_x((1, 3)))]
    ppermute x27, waiting for transfers between devices: 62.3 us -> 69.3 us  [move(): return lax.ppermute(array, BOTH, across(major, mask))]
    ppermute x3, waiting for transfers between devices: 16.4 us -> 9.51 us  [gather_x(): other = lax.ppermute(block, 'gy', across_x((1, 3)))]
    ppermute x3, starting transfers between devices: 8.59 us -> 3.01 us  [gather_x(): lax.ppermute(jnp.concatenate([block, other]), 'gy', across_x((3, 1)))]
  transfers between devices with their start and end apart: 43 -> 43, of which waited for: 24 -> 30; matrix products, arithmetic and copies ran while one was open for 4% -> 3% of each run, Pallas kernels for 21% -> 17%
where the time goes in v2:
time: 247 us
  waiting for transfers between devices  110 us (45%)
  starting transfers between devices  49.8 us (20%)
  Pallas kernels  42.5 us (17%)
  local copies, waits for them, and re-layouts  20.4 us (8%)
  between operations  15.3 us (6%)
  other arithmetic  7.03 us (3%)
    ppermute x27, waiting for transfers between devices, move(): return lax.ppermute(array, BOTH, across(major, mask))  69.3 us
    ppermute x27, starting transfers between devices, move(): return lax.ppermute(array, BOTH, across(major, mask))  39.6 us
    pallas_call x2, Pallas kernels, gate_and_up(): pl.pallas_call(kernel, in_specs=[SMEM] + [VMEM] * 4 + [HBM] * 2, out_spec...  26.5 us
    unnamed x38, local copies, waits for them, and re-layouts  19 us
    pallas_call x3, Pallas kernels, project(): pl.pallas_call(kernel, in_specs=[SMEM] + [VMEM] * (len(blocks) + 1), out_...  14.4 us
    ppermute x2, waiting for transfers between devices, sum_over_x(): other = lax.ppermute(other, 'gy', across_x((1, 3)))  12.3 us
    ppermute x3, waiting for transfers between devices, gather_x(): lax.ppermute(jnp.concatenate([block, other]), 'gy', across_x((3, 1)))  11.3 us
    ppermute x3, waiting for transfers between devices, gather_x(): other = lax.ppermute(block, 'gy', across_x((1, 3)))  9.51 us
  transfers between devices with their start and end apart: 43, of which 30 were waited for; matrix products, arithmetic and copies ran while one was open for 3% of the time, Pallas kernels for 17%

profile of v2, /device:TPU:0, one launch (start us, length us, event | category | flops | bytes accessed | tf_op | source)
XLA Modules:
  0.0 246.6 jit_solution(6831902444862525992)
XLA Ops:
  17.5 2.9 %collective-permute-start.1 = (bf16[256,1024]{1,0:T(8,128)(2,1)S(1)}, bf16[256,1024]{1,0:T(8,128)(2,1)S(1)}, u32[]{:S(2)}, u32[]{:S(2)}) collective-permute-start(bf16[256,1024]{1,0:T(8,128)(2,1)S(1)} %pad_maximum_fusion.5), channel_id=1, source_target_pairs={{0,6},{1,3},{2,4},{3,1},{4,2},{5,7},{6,0},{7,5},{8,14},{9,11},{10,... | collective-permute-start | bytes 1572872 | tf_op jit(solution)/shard_map/ppermute | solution.py:91
  20.4 7.6 %collective-permute-done.1.refs_2_ = bf16[256,1024]{1,0:T(8,128)(2,1)S(1)} collective-permute-done((bf16[256,1024]{1,0:T(8,128)(2,1)S(1)}, bf16[256,1024]{1,0:T(8,128)(2,1)S(1)}, u32[]{:S(2)}, u32[]{:S(2)}) %collective-permute-start.1) | collective-permute-done | bytes 524320 | tf_op jit(solution)/shard_map/ppermute | solution.py:91
  30.8 3.4 %copy-done.8 = bf16[1024,2048]{1,0:T(8,128)(2,1)S(1)} copy-done((bf16[1024,2048]{1,0:T(8,128)(2,1)S(1)}, bf16[1024,2048]{1,0:T(8,128)(2,1)}, u32[]{:S(2)}) %copy-start.8) | copy-done | bytes 4194328
  34.3 5.2 %shard_map.110 = (bf16[256,2048]{1,0:T(8,128)(2,1)S(1)}, bf16[256,2048]{1,0:T(8,128)(2,1)S(1)}, bf16[256,2048]{1,0:T(8,128)(2,1)S(1)}, bf16[256,2048]{1,0:T(8,128)(2,1)S(1)}) custom-call(s32[16]{0:T(128)S(1)} %select_n.91.places, bf16[128,1024]{1,0:T(8,128)(2,1)S(1)} %copy.44.refs_0_, bf16[128,1024]{1,0:T(8,128)(2,1)S(1)} %collective-permute-done.refs_1_, ...), custom_call_target="tpu_custom_call" | custom-call | flops 4294967296 | bytes 4194304 | tf_op jit(solution)/shard_map/pallas_call | solution.py:176
  39.4 3.8 %collective-permute-start.3 = (bf16[256,2048]{1,0:T(8,128)(2,1)S(1)}, bf16[256,2048]{1,0:T(8,128)(2,1)S(1)}, u32[]{:S(2)}, u32[]{:S(2)}) collective-permute-start(bf16[256,2048]{1,0:T(8,128)(2,1)S(1)} %get-tuple-element.33), channel_id=1, source_target_pairs={{0,16},{1,65},{2,18},{3,67},{4,20},{5,69},{6,22},{7,71},{8,24},{9,... | collective-permute-start | bytes 3145736 | tf_op jit(solution)/shard_map/ppermute | solution.py:79
  44.8 11.3 %collective-permute-done.3 = bf16[256,2048]{1,0:T(8,128)(2,1)S(1)} collective-permute-done((bf16[256,2048]{1,0:T(8,128)(2,1)S(1)}, bf16[256,2048]{1,0:T(8,128)(2,1)S(1)}, u32[]{:S(2)}, u32[]{:S(2)}) %collective-permute-start.3) | collective-permute-done | bytes 1048608 | tf_op jit(solution)/shard_map/ppermute | solution.py:79
  56.1 12.8 %collective-permute-done.4 = bf16[256,2048]{1,0:T(8,128)(2,1)S(1)} collective-permute-done((bf16[256,2048]{1,0:T(8,128)(2,1)S(1)}, bf16[256,2048]{1,0:T(8,128)(2,1)S(1)}, u32[]{:S(2)}, u32[]{:S(2)}) %collective-permute-start.4) | collective-permute-done | bytes 1048608 | tf_op jit(solution)/shard_map/ppermute | solution.py:79
  71.1 3.1 %collective-permute-start.6 = (bf16[64,2048]{1,0:T(8,128)(2,1)}, bf16[64,2048]{1,0:T(8,128)(2,1)}, u32[]{:S(2)}, u32[]{:S(2)}) collective-permute-start(bf16[64,2048]{1,0:T(8,128)(2,1)} %get-tuple-element.60), channel_id=1, source_target_pairs={{0,64},{1,17},{2,66},{3,19},{4,68},{5,21},{6,70},{7,23},{8,72},{9,... | collective-permute-start | bytes 786440 | tf_op jit(solution)/shard_map/ppermute | solution.py:79
  75.3 4.0 %collective-permute-done.6 = bf16[64,2048]{1,0:T(8,128)(2,1)} collective-permute-done((bf16[64,2048]{1,0:T(8,128)(2,1)}, bf16[64,2048]{1,0:T(8,128)(2,1)}, u32[]{:S(2)}, u32[]{:S(2)}) %collective-permute-start.6) | collective-permute-done | bytes 262176 | tf_op jit(solution)/shard_map/ppermute | solution.py:79
  79.3 3.2 %collective-permute-done.7 = bf16[64,2048]{1,0:T(8,128)(2,1)} collective-permute-done((bf16[64,2048]{1,0:T(8,128)(2,1)}, bf16[64,2048]{1,0:T(8,128)(2,1)}, u32[]{:S(2)}, u32[]{:S(2)}) %collective-permute-start.7) | collective-permute-done | bytes 262176 | tf_op jit(solution)/shard_map/ppermute | solution.py:79
  88.4 2.8 %collective-permute-start.11 = (bf16[32,4224]{1,0:T(8,128)(2,1)S(1)}, bf16[32,4224]{1,0:T(8,128)(2,1)S(1)}, u32[]{:S(2)}, u32[]{:S(2)}) collective-permute-start(bf16[32,4224]{1,0:T(8,128)(2,1)S(1)} %fusion.8), channel_id=1, source_target_pairs={{0,64},{1,17},{2,66},{3,19},{4,68},{5,21},{6,70},{7,23},{8,72},{9,... | collective-permute-start | bytes 811016 | tf_op jit(solution)/shard_map/ppermute | solution.py:79
  93.7 4.9 %collective-permute-done.11 = bf16[32,4224]{1,0:T(8,128)(2,1)S(1)} collective-permute-done((bf16[32,4224]{1,0:T(8,128)(2,1)S(1)}, bf16[32,4224]{1,0:T(8,128)(2,1)S(1)}, u32[]{:S(2)}, u32[]{:S(2)}) %collective-permute-start.11) | collective-permute-done | bytes 270368 | tf_op jit(solution)/shard_map/ppermute | solution.py:79
  98.6 2.8 %collective-permute-done.12 = bf16[32,4224]{1,0:T(8,128)(2,1)S(1)} collective-permute-done((bf16[32,4224]{1,0:T(8,128)(2,1)S(1)}, bf16[32,4224]{1,0:T(8,128)(2,1)S(1)}, u32[]{:S(2)}, u32[]{:S(2)}) %collective-permute-start.12) | collective-permute-done | bytes 270368 | tf_op jit(solution)/shard_map/ppermute | solution.py:79
  102.5 3.1 %collective-permute-start.14 = (bf16[64,4224]{1,0:T(8,128)(2,1)S(1)}, bf16[64,4224]{1,0:T(8,128)(2,1)S(1)}, u32[]{:S(2)}, u32[]{:S(2)}) collective-permute-start(bf16[64,4224]{1,0:T(8,128)(2,1)S(1)} %pad_maximum_fusion.3.refs_0_), channel_id=1, source_target_pairs={{0,16},{1,65},{2,18},{3,67},{4,20},{5,69},{6,22},{7,71},{8,24},{9,... | collective-permute-start | bytes 1622024 | tf_op jit(solution)/shard_map/ppermute | solution.py:79
  106.4 4.1 %collective-permute-start.18 = (bf16[64,4224]{1,0:T(8,128)(2,1)S(1)}, bf16[64,4224]{1,0:T(8,128)(2,1)S(1)}, u32[]{:S(2)}, u32[]{:S(2)}) collective-permute-start(bf16[64,4224]{1,0:T(8,128)(2,1)S(1)} %pad_maximum_fusion.4.refs_0_), channel_id=1, source_target_pairs={{0,16},{1,65},{2,18},{3,67},{4,20},{5,69},{6,22},{7,71},{8,24},{9,... | collective-permute-start | bytes 1622024 | tf_op jit(solution)/shard_map/ppermute | solution.py:79
  113.5 5.3 %collective-permute-done.14.refs_2_ = bf16[64,4224]{1,0:T(8,128)(2,1)S(1)} collective-permute-done((bf16[64,4224]{1,0:T(8,128)(2,1)S(1)}, bf16[64,4224]{1,0:T(8,128)(2,1)S(1)}, u32[]{:S(2)}, u32[]{:S(2)}) %collective-permute-start.14) | collective-permute-done | bytes 540704 | tf_op jit(solution)/shard_map/ppermute | solution.py:79
  118.8 3.2 %collective-permute-done.15.refs_3_ = bf16[64,4224]{1,0:T(8,128)(2,1)} collective-permute-done((bf16[64,4224]{1,0:T(8,128)(2,1)S(1)}, bf16[64,4224]{1,0:T(8,128)(2,1)}, u32[]{:S(2)}, u32[]{:S(2)}) %collective-permute-start.15) | collective-permute-done | bytes 540704 | tf_op jit(solution)/shard_map/ppermute | solution.py:79
  122.1 13.2 %shard_map.111 = (bf16[128,3456]{1,0:T(8,128)(2,1)}, bf16[128,3456]{1,0:T(8,128)(2,1)}) custom-call(s32[4]{0:T(128)S(1)} %compare_select_fusion.2.places, bf16[64,4224]{1,0:T(8,128)(2,1)S(1)} %pad_maximum_fusion.3.refs_0_, bf16[64,4224]{1,0:T(8,128)(2,1)S(1)} %collective-permute-done.13.refs_1_, bf16[64,4224]{1,0:T(8,128)(2,1)S(1)} %collective-permute-done.14.refs_2_, ...), custom_call_target="tpu_custom_call" | custom-call | flops 6979321856 | bytes 27262976 | tf_op jit(solution)/shard_map/pallas_call | solution.py:261
  135.3 2.8 %collective-permute-start.16 = (bf16[128,3456]{1,0:T(8,128)(2,1)}, bf16[128,3456]{1,0:T(8,128)(2,1)S(1)}, u32[]{:S(2)}, u32[]{:S(2)}) collective-permute-start(bf16[128,3456]{1,0:T(8,128)(2,1)} %get-tuple-element.37), channel_id=1, source_target_pairs={{0,6},{1,3},{2,4},{3,1},{4,2},{5,7},{6,0},{7,5},{8,14},{9,11},{10,... | collective-permute-start | bytes 2654216 | tf_op jit(solution)/shard_map/ppermute | solution.py:280
  138.1 13.3 %shard_map.112 = (bf16[128,3456]{1,0:T(8,128)(2,1)}, bf16[128,3456]{1,0:T(8,128)(2,1)}) custom-call(s32[4]{0:T(128)S(1)} %compare_select_fusion.2.places, bf16[64,4224]{1,0:T(8,128)(2,1)S(1)} %pad_maximum_fusion.4.refs_0_, bf16[64,4224]{1,0:T(8,128)(2,1)S(1)} %collective-permute-done.17.refs_1_, bf16[64,4224]{1,0:T(8,128)(2,1)S(1)} %collective-permute-done.18.refs_2_, ...), custom_call_target="tpu_custom_call" | custom-call | flops 6979321856 | bytes 27262976 | tf_op jit(solution)/shard_map/pallas_call | solution.py:261
  153.7 2.9 %copy-done.2 = bf16[1664,2048]{1,0:T(8,128)(2,1)S(1)} copy-done((bf16[1664,2048]{1,0:T(8,128)(2,1)S(1)}, bf16[1664,2048]{1,0:T(8,128)(2,1)}, u32[]{:S(2)}) %copy-start.2) | copy-done | bytes 6815768
  160.6 5.0 %collective-permute-done.20 = bf16[64,3456]{1,0:T(8,128)(2,1)S(1)} collective-permute-done((bf16[64,3456]{1,0:T(8,128)(2,1)S(1)}, bf16[64,3456]{1,0:T(8,128)(2,1)S(1)}, u32[]{:S(2)}, u32[]{:S(2)}) %collective-permute-start.20) | collective-permute-done | bytes 442400 | tf_op jit(solution)/shard_map/ppermute | solution.py:282
  166.2 3.1 %collective-permute-done.30 = bf16[128,3456]{1,0:T(8,128)(2,1)S(1)} collective-permute-done((bf16[128,3456]{1,0:T(8,128)(2,1)}, bf16[128,3456]{1,0:T(8,128)(2,1)S(1)}, u32[]{:S(2)}, u32[]{:S(2)}) %collective-permute-start.30) | collective-permute-done | bytes 884768 | tf_op jit(solution)/shard_map/ppermute | solution.py:280
  170.4 3.6 %collective-permute-done.21.refs_1_ = bf16[64,1664]{1,0:T(8,128)(2,1)S(1)} collective-permute-done((bf16[64,1664]{1,0:T(8,128)(2,1)S(1)}, bf16[64,1664]{1,0:T(8,128)(2,1)S(1)}, u32[]{:S(2)}, u32[]{:S(2)}) %collective-permute-start.21) | collective-permute-done | bytes 213024 | tf_op jit(solution)/shard_map/ppermute | solution.py:88
  174.1 7.2 %collective-permute-done.31 = bf16[64,3456]{1,0:T(8,128)(2,1)S(1)} collective-permute-done((bf16[64,3456]{1,0:T(8,128)(2,1)S(1)}, bf16[64,3456]{1,0:T(8,128)(2,1)S(1)}, u32[]{:S(2)}, u32[]{:S(2)}) %collective-permute-start.31) | collective-permute-done | bytes 442400 | tf_op jit(solution)/shard_map/ppermute | solution.py:282
  184.0 5.8 %collective-permute-done.32.refs_1_ = bf16[64,1664]{1,0:T(8,128)(2,1)S(1)} collective-permute-done((bf16[64,1664]{1,0:T(8,128)(2,1)S(1)}, bf16[64,1664]{1,0:T(8,128)(2,1)S(1)}, u32[]{:S(2)}, u32[]{:S(2)}) %collective-permute-start.32) | collective-permute-done | bytes 213024 | tf_op jit(solution)/shard_map/ppermute | solution.py:88
  190.7 2.9 %copy-done.4 = bf16[1664,2048]{1,0:T(8,128)(2,1)S(1)} copy-done((bf16[1664,2048]{1,0:T(8,128)(2,1)S(1)}, bf16[1664,2048]{1,0:T(8,128)(2,1)}, u32[]{:S(2)}) %copy-start.4) | copy-done | bytes 6815768
  193.6 4.6 %shard_map.114 = (bf16[128,2048]{1,0:T(8,128)(2,1)S(1)}, bf16[128,2048]{1,0:T(8,128)(2,1)S(1)}, bf16[128,2048]{1,0:T(8,128)(2,1)S(1)}, bf16[128,2048]{1,0:T(8,128)(2,1)S(1)}) custom-call(s32[32]{0:T(128)S(1)} %reshape.426.places, bf16[64,1664]{1,0:T(8,128)(2,1)S(1)} %multiply_convert_fusion.1.refs_0_, bf16[64,1664]{1,0:T(8,128)(2,1)S(1)} %collective-permute-done.21.refs_1_, ...), custom_call_target="tpu_custom_call" | custom-call | flops 3489660928 | bytes 6815744 | tf_op jit(solution)/shard_map/pallas_call | solution.py:176
  201.6 2.9 %collective-permute-start.26 = (bf16[128,2048]{1,0:T(8,128)(2,1)S(1)}, bf16[128,2048]{1,0:T(8,128)(2,1)S(1)}, u32[]{:S(2)}, u32[]{:S(2)}) collective-permute-start(bf16[128,2048]{1,0:T(8,128)(2,1)S(1)} %get-tuple-element.45), channel_id=1, source_target_pairs={{0,24},{1,97},{2,26},{3,99},{4,28},{5,101},{6,30},{7,103},{8,16},{... | collective-permute-start | bytes 1572872 | tf_op jit(solution)/shard_map/ppermute | solution.py:79
  204.4 4.7 %shard_map.115 = (bf16[128,2048]{1,0:T(8,128)(2,1)S(1)}, bf16[128,2048]{1,0:T(8,128)(2,1)S(1)}, bf16[128,2048]{1,0:T(8,128)(2,1)S(1)}, bf16[128,2048]{1,0:T(8,128)(2,1)S(1)}) custom-call(s32[32]{0:T(128)S(1)} %reshape.426.places, bf16[64,1664]{1,0:T(8,128)(2,1)S(1)} %fusion.6.refs_0_, bf16[64,1664]{1,0:T(8,128)(2,1)S(1)} %collective-permute-done.32.refs_1_, ...), custom_call_target="tpu_custom_call" | custom-call | flops 3489660928 | bytes 6815744 | tf_op jit(solution)/shard_map/pallas_call | solution.py:176
  218.4 5.6 %collective-permute-done.35 = bf16[128,2048]{1,0:T(8,128)(2,1)S(1)} collective-permute-done((bf16[128,2048]{1,0:T(8,128)(2,1)S(1)}, bf16[128,2048]{1,0:T(8,128)(2,1)S(1)}, u32[]{:S(2)}, u32[]{:S(2)}) %collective-permute-start.35) | collective-permute-done | bytes 524320 | tf_op jit(solution)/shard_map/ppermute | solution.py:79
  224.5 4.0 %collective-permute-done.36 = bf16[128,2048]{1,0:T(8,128)(2,1)S(1)} collective-permute-done((bf16[128,2048]{1,0:T(8,128)(2,1)S(1)}, bf16[128,2048]{1,0:T(8,128)(2,1)S(1)}, u32[]{:S(2)}, u32[]{:S(2)}) %collective-permute-start.36) | collective-permute-done | bytes 524320 | tf_op jit(solution)/shard_map/ppermute | solution.py:79
  (164 shorter events, 66.4 us)
Async XLA Ops:
  6.5 115.5 %all-gather.3.cloned.1.call-start = ((), (), s32[]{:S(2)}) async-start(), calls=%async_computation | async-start | bytes 20447232 | tf_op jit(solution)/shard_map/all_gather | solution.py:300
  7.3 114.8 %all-gather.5.cloned.1.call-start = ((), (), s32[]{:S(2)}) async-start(), calls=%async_computation.1 | async-start | bytes 20447232 | tf_op jit(solution)/shard_map/all_gather | solution.py:301
  17.5 10.5 %collective-permute-start.1 = (bf16[256,1024]{1,0:T(8,128)(2,1)S(1)}, bf16[256,1024]{1,0:T(8,128)(2,1)S(1)}, u32[]{:S(2)}, u32[]{:S(2)}) collective-permute-start(bf16[256,1024]{1,0:T(8,128)(2,1)S(1)} %pad_maximum_fusion.5), channel_id=1, source_target_pairs={{0,6},{1,3},{2,4},{3,1},{4,2},{5,7},{6,0},{7,5},{8,14},{9,11},{10,... | collective-permute-start | bytes 1572872 | tf_op jit(solution)/shard_map/ppermute | solution.py:91
  39.4 16.6 %collective-permute-start.3 = (bf16[256,2048]{1,0:T(8,128)(2,1)S(1)}, bf16[256,2048]{1,0:T(8,128)(2,1)S(1)}, u32[]{:S(2)}, u32[]{:S(2)}) collective-permute-start(bf16[256,2048]{1,0:T(8,128)(2,1)S(1)} %get-tuple-element.33), channel_id=1, source_target_pairs={{0,16},{1,65},{2,18},{3,67},{4,20},{5,69},{6,22},{7,71},{8,24},{9,... | collective-permute-start | bytes 3145736 | tf_op jit(solution)/shard_map/ppermute | solution.py:79
  43.2 25.6 %collective-permute-start.4 = (bf16[256,2048]{1,0:T(8,128)(2,1)S(1)}, bf16[256,2048]{1,0:T(8,128)(2,1)S(1)}, u32[]{:S(2)}, u32[]{:S(2)}) collective-permute-start(bf16[256,2048]{1,0:T(8,128)(2,1)S(1)} %get-tuple-element.34), channel_id=1, source_target_pairs={{0,8},{1,33},{2,10},{3,35},{4,12},{5,37},{6,14},{7,39},{8,0},{9,41... | collective-permute-start | bytes 3145736 | tf_op jit(solution)/shard_map/ppermute | solution.py:79
  44.8 24.1 %collective-permute-start.5 = (bf16[256,2048]{1,0:T(8,128)(2,1)S(1)}, bf16[256,2048]{1,0:T(8,128)(2,1)S(1)}, u32[]{:S(2)}, u32[]{:S(2)}) collective-permute-start(bf16[256,2048]{1,0:T(8,128)(2,1)S(1)} %get-tuple-element.35), channel_id=1, source_target_pairs={{0,24},{1,97},{2,26},{3,99},{4,28},{5,101},{6,30},{7,103},{8,16},{... | collective-permute-start | bytes 3145736 | tf_op jit(solution)/shard_map/ppermute | solution.py:79
  71.1 8.2 %collective-permute-start.6 = (bf16[64,2048]{1,0:T(8,128)(2,1)}, bf16[64,2048]{1,0:T(8,128)(2,1)}, u32[]{:S(2)}, u32[]{:S(2)}) collective-permute-start(bf16[64,2048]{1,0:T(8,128)(2,1)} %get-tuple-element.60), channel_id=1, source_target_pairs={{0,64},{1,17},{2,66},{3,19},{4,68},{5,21},{6,70},{7,23},{8,72},{9,... | collective-permute-start | bytes 786440 | tf_op jit(solution)/shard_map/ppermute | solution.py:79
  74.3 8.2 %collective-permute-start.7 = (bf16[64,2048]{1,0:T(8,128)(2,1)}, bf16[64,2048]{1,0:T(8,128)(2,1)}, u32[]{:S(2)}, u32[]{:S(2)}) collective-permute-start(bf16[64,2048]{1,0:T(8,128)(2,1)} %get-tuple-element.62), channel_id=1, source_target_pairs={{0,32},{1,9},{2,34},{3,11},{4,36},{5,13},{6,38},{7,15},{8,40},{9,1... | collective-permute-start | bytes 786440 | tf_op jit(solution)/shard_map/ppermute | solution.py:79
  88.4 10.2 %collective-permute-start.11 = (bf16[32,4224]{1,0:T(8,128)(2,1)S(1)}, bf16[32,4224]{1,0:T(8,128)(2,1)S(1)}, u32[]{:S(2)}, u32[]{:S(2)}) collective-permute-start(bf16[32,4224]{1,0:T(8,128)(2,1)S(1)} %fusion.8), channel_id=1, source_target_pairs={{0,64},{1,17},{2,66},{3,19},{4,68},{5,21},{6,70},{7,23},{8,72},{9,... | collective-permute-start | bytes 811016 | tf_op jit(solution)/shard_map/ppermute | solution.py:79
  91.1 10.2 %collective-permute-start.12 = (bf16[32,4224]{1,0:T(8,128)(2,1)S(1)}, bf16[32,4224]{1,0:T(8,128)(2,1)S(1)}, u32[]{:S(2)}, u32[]{:S(2)}) collective-permute-start(bf16[32,4224]{1,0:T(8,128)(2,1)S(1)} %fusion.8), channel_id=1, source_target_pairs={{0,96},{1,25},{2,98},{3,27},{4,100},{5,29},{6,102},{7,31},{8,104},... | collective-permute-start | bytes 811016 | tf_op jit(solution)/shard_map/ppermute | solution.py:79
  101.4 9.4 %collective-permute-start.13 = (bf16[64,4224]{1,0:T(8,128)(2,1)S(1)}, bf16[64,4224]{1,0:T(8,128)(2,1)S(1)}, u32[]{:S(2)}, u32[]{:S(2)}) collective-permute-start(bf16[64,4224]{1,0:T(8,128)(2,1)S(1)} %pad_maximum_fusion.3.refs_0_), channel_id=1, source_target_pairs={{0,8},{1,33},{2,10},{3,35},{4,12},{5,37},{6,14},{7,39},{8,0},{9,41... | collective-permute-start | bytes 1622024 | tf_op jit(solution)/shard_map/ppermute | solution.py:79
  102.5 16.3 %collective-permute-start.14 = (bf16[64,4224]{1,0:T(8,128)(2,1)S(1)}, bf16[64,4224]{1,0:T(8,128)(2,1)S(1)}, u32[]{:S(2)}, u32[]{:S(2)}) collective-permute-start(bf16[64,4224]{1,0:T(8,128)(2,1)S(1)} %pad_maximum_fusion.3.refs_0_), channel_id=1, source_target_pairs={{0,16},{1,65},{2,18},{3,67},{4,20},{5,69},{6,22},{7,71},{8,24},{9,... | collective-permute-start | bytes 1622024 | tf_op jit(solution)/shard_map/ppermute | solution.py:79
  105.6 16.5 %collective-permute-start.15 = (bf16[64,4224]{1,0:T(8,128)(2,1)S(1)}, bf16[64,4224]{1,0:T(8,128)(2,1)}, u32[]{:S(2)}, u32[]{:S(2)}) collective-permute-start(bf16[64,4224]{1,0:T(8,128)(2,1)S(1)} %pad_maximum_fusion.3.refs_0_), channel_id=1, source_target_pairs={{0,24},{1,97},{2,26},{3,99},{4,28},{5,101},{6,30},{7,103},{8,16},{... | collective-permute-start | bytes 1622024 | tf_op jit(solution)/shard_map/ppermute | solution.py:79
  106.3 31.9 %collective-permute-start.17 = (bf16[64,4224]{1,0:T(8,128)(2,1)S(1)}, bf16[64,4224]{1,0:T(8,128)(2,1)S(1)}, u32[]{:S(2)}, u32[]{:S(2)}) collective-permute-start(bf16[64,4224]{1,0:T(8,128)(2,1)S(1)} %pad_maximum_fusion.4.refs_0_), channel_id=1, source_target_pairs={{0,8},{1,33},{2,10},{3,35},{4,12},{5,37},{6,14},{7,39},{8,0},{9,41... | collective-permute-start | bytes 1622024 | tf_op jit(solution)/shard_map/ppermute | solution.py:79
  106.4 31.8 %collective-permute-start.18 = (bf16[64,4224]{1,0:T(8,128)(2,1)S(1)}, bf16[64,4224]{1,0:T(8,128)(2,1)S(1)}, u32[]{:S(2)}, u32[]{:S(2)}) collective-permute-start(bf16[64,4224]{1,0:T(8,128)(2,1)S(1)} %pad_maximum_fusion.4.refs_0_), channel_id=1, source_target_pairs={{0,16},{1,65},{2,18},{3,67},{4,20},{5,69},{6,22},{7,71},{8,24},{9,... | collective-permute-start | bytes 1622024 | tf_op jit(solution)/shard_map/ppermute | solution.py:79
  110.9 27.3 %collective-permute-start.19 = (bf16[64,4224]{1,0:T(8,128)(2,1)S(1)}, bf16[64,4224]{1,0:T(8,128)(2,1)}, u32[]{:S(2)}, u32[]{:S(2)}) collective-permute-start(bf16[64,4224]{1,0:T(8,128)(2,1)S(1)} %pad_maximum_fusion.4.refs_0_), channel_id=1, source_target_pairs={{0,24},{1,97},{2,26},{3,99},{4,28},{5,101},{6,30},{7,103},{8,16},{... | collective-permute-start | bytes 1622024 | tf_op jit(solution)/shard_map/ppermute | solution.py:79
  135.3 16.2 %collective-permute-start.16 = (bf16[128,3456]{1,0:T(8,128)(2,1)}, bf16[128,3456]{1,0:T(8,128)(2,1)S(1)}, u32[]{:S(2)}, u32[]{:S(2)}) collective-permute-start(bf16[128,3456]{1,0:T(8,128)(2,1)} %get-tuple-element.37), channel_id=1, source_target_pairs={{0,6},{1,3},{2,4},{3,1},{4,2},{5,7},{6,0},{7,5},{8,14},{9,11},{10,... | collective-permute-start | bytes 2654216 | tf_op jit(solution)/shard_map/ppermute | solution.py:280
  152.5 13.1 %collective-permute-start.20 = (bf16[64,3456]{1,0:T(8,128)(2,1)S(1)}, bf16[64,3456]{1,0:T(8,128)(2,1)S(1)}, u32[]{:S(2)}, u32[]{:S(2)}) collective-permute-start(bf16[64,3456]{1,0:T(8,128)(2,1)S(1)} %add_convert_fusion.1), channel_id=1, source_target_pairs={{0,2},{1,7},{2,0},{3,5},{4,6},{5,3},{6,4},{7,1},{8,10},{9,15},{10,... | collective-permute-start | bytes 1327112 | tf_op jit(solution)/shard_map/ppermute | solution.py:282
  152.5 16.8 %collective-permute-start.30 = (bf16[128,3456]{1,0:T(8,128)(2,1)}, bf16[128,3456]{1,0:T(8,128)(2,1)S(1)}, u32[]{:S(2)}, u32[]{:S(2)}) collective-permute-start(bf16[128,3456]{1,0:T(8,128)(2,1)} %get-tuple-element.38), channel_id=1, source_target_pairs={{0,6},{1,3},{2,4},{3,1},{4,2},{5,7},{6,0},{7,5},{8,14},{9,11},{10,... | collective-permute-start | bytes 2654216 | tf_op jit(solution)/shard_map/ppermute | solution.py:280
  166.1 7.9 %collective-permute-start.21 = (bf16[64,1664]{1,0:T(8,128)(2,1)S(1)}, bf16[64,1664]{1,0:T(8,128)(2,1)S(1)}, u32[]{:S(2)}, u32[]{:S(2)}) collective-permute-start(bf16[64,1664]{1,0:T(8,128)(2,1)S(1)} %multiply_convert_fusion.1.refs_0_), channel_id=1, source_target_pairs={{0,2},{1,7},{2,0},{3,5},{4,6},{5,3},{6,4},{7,1},{8,10},{9,15},{10,... | collective-permute-start | bytes 638984 | tf_op jit(solution)/shard_map/ppermute | solution.py:88
  169.5 11.9 %collective-permute-start.31 = (bf16[64,3456]{1,0:T(8,128)(2,1)S(1)}, bf16[64,3456]{1,0:T(8,128)(2,1)S(1)}, u32[]{:S(2)}, u32[]{:S(2)}) collective-permute-start(bf16[64,3456]{1,0:T(8,128)(2,1)S(1)} %add_convert_fusion), channel_id=1, source_target_pairs={{0,2},{1,7},{2,0},{3,5},{4,6},{5,3},{6,4},{7,1},{8,10},{9,15},{10,... | collective-permute-start | bytes 1327112 | tf_op jit(solution)/shard_map/ppermute | solution.py:282
  174.0 9.4 %collective-permute-start.22 = (bf16[128,1664]{1,0:T(8,128)(2,1)S(1)}, bf16[128,1664]{1,0:T(8,128)(2,1)S(1)}, u32[]{:S(2)}, u32[]{:S(2)}) collective-permute-start(bf16[128,1664]{1,0:T(8,128)(2,1)S(1)} %pad_maximum_fusion.6), channel_id=1, source_target_pairs={{0,6},{1,3},{2,4},{3,1},{4,2},{5,7},{6,0},{7,5},{8,14},{9,11},{10,... | collective-permute-start | bytes 1277960 | tf_op jit(solution)/shard_map/ppermute | solution.py:91
  190.5 9.5 %collective-permute-start.33 = (bf16[128,1664]{1,0:T(8,128)(2,1)}, bf16[128,1664]{1,0:T(8,128)(2,1)S(1)}, u32[]{:S(2)}, u32[]{:S(2)}) collective-permute-start(bf16[128,1664]{1,0:T(8,128)(2,1)} %pad_maximum_fusion.7), channel_id=1, source_target_pairs={{0,6},{1,3},{2,4},{3,1},{4,2},{5,7},{6,0},{7,5},{8,14},{9,11},{10,... | collective-permute-start | bytes 1277960 | tf_op jit(solution)/shard_map/ppermute | solution.py:91
  200.3 10.9 %collective-permute-start.24 = (bf16[128,2048]{1,0:T(8,128)(2,1)S(1)}, bf16[128,2048]{1,0:T(8,128)(2,1)S(1)}, u32[]{:S(2)}, u32[]{:S(2)}) collective-permute-start(bf16[128,2048]{1,0:T(8,128)(2,1)S(1)} %get-tuple-element.43), channel_id=1, source_target_pairs={{0,16},{1,65},{2,18},{3,67},{4,20},{5,69},{6,22},{7,71},{8,24},{9,... | collective-permute-start | bytes 1572872 | tf_op jit(solution)/shard_map/ppermute | solution.py:79
  200.4 14.0 %collective-permute-start.25 = (bf16[128,2048]{1,0:T(8,128)(2,1)S(1)}, bf16[128,2048]{1,0:T(8,128)(2,1)S(1)}, u32[]{:S(2)}, u32[]{:S(2)}) collective-permute-start(bf16[128,2048]{1,0:T(8,128)(2,1)S(1)} %get-tuple-element.44), channel_id=1, source_target_pairs={{0,8},{1,33},{2,10},{3,35},{4,12},{5,37},{6,14},{7,39},{8,0},{9,41... | collective-permute-start | bytes 1572872 | tf_op jit(solution)/shard_map/ppermute | solution.py:79
  201.6 15.1 %collective-permute-start.26 = (bf16[128,2048]{1,0:T(8,128)(2,1)S(1)}, bf16[128,2048]{1,0:T(8,128)(2,1)S(1)}, u32[]{:S(2)}, u32[]{:S(2)}) collective-permute-start(bf16[128,2048]{1,0:T(8,128)(2,1)S(1)} %get-tuple-element.45), channel_id=1, source_target_pairs={{0,24},{1,97},{2,26},{3,99},{4,28},{5,101},{6,30},{7,103},{8,16},{... | collective-permute-start | bytes 1572872 | tf_op jit(solution)/shard_map/ppermute | solution.py:79
  209.1 14.9 %collective-permute-start.35 = (bf16[128,2048]{1,0:T(8,128)(2,1)S(1)}, bf16[128,2048]{1,0:T(8,128)(2,1)S(1)}, u32[]{:S(2)}, u32[]{:S(2)}) collective-permute-start(bf16[128,2048]{1,0:T(8,128)(2,1)S(1)} %get-tuple-element.52), channel_id=1, source_target_pairs={{0,16},{1,65},{2,18},{3,67},{4,20},{5,69},{6,22},{7,71},{8,24},{9,... | collective-permute-start | bytes 1572872 | tf_op jit(solution)/shard_map/ppermute | solution.py:79
  209.3 19.2 %collective-permute-start.36 = (bf16[128,2048]{1,0:T(8,128)(2,1)S(1)}, bf16[128,2048]{1,0:T(8,128)(2,1)S(1)}, u32[]{:S(2)}, u32[]{:S(2)}) collective-permute-start(bf16[128,2048]{1,0:T(8,128)(2,1)S(1)} %get-tuple-element.53), channel_id=1, source_target_pairs={{0,8},{1,33},{2,10},{3,35},{4,12},{5,37},{6,14},{7,39},{8,0},{9,41... | collective-permute-start | bytes 1572872 | tf_op jit(solution)/shard_map/ppermute | solution.py:79
  211.1 19.6 %collective-permute-start.37 = (bf16[128,2048]{1,0:T(8,128)(2,1)S(1)}, bf16[128,2048]{1,0:T(8,128)(2,1)S(1)}, u32[]{:S(2)}, u32[]{:S(2)}) collective-permute-start(bf16[128,2048]{1,0:T(8,128)(2,1)S(1)} %get-tuple-element.54), channel_id=1, source_target_pairs={{0,24},{1,97},{2,26},{3,99},{4,28},{5,101},{6,30},{7,103},{8,16},{... | collective-permute-start | bytes 1572872 | tf_op jit(solution)/shard_map/ppermute | solution.py:79
  216.9 15.5 %collective-permute-start.27 = (bf16[32,2048]{1,0:T(8,128)(2,1)S(1)}, bf16[32,2048]{1,0:T(8,128)(2,1)S(1)}, u32[]{:S(2)}, u32[]{:S(2)}) collective-permute-start(bf16[32,2048]{1,0:T(8,128)(2,1)S(1)} %get-tuple-element.63), channel_id=1, source_target_pairs={{0,64},{1,17},{2,66},{3,19},{4,68},{5,21},{6,70},{7,23},{8,72},{9,... | collective-permute-start | bytes 393224 | tf_op jit(solution)/shard_map/ppermute | solution.py:79
  217.2 17.9 %collective-permute-start.28 = (bf16[32,2048]{1,0:T(8,128)(2,1)S(1)}, bf16[32,2048]{1,0:T(8,128)(2,1)S(1)}, u32[]{:S(2)}, u32[]{:S(2)}) collective-permute-start(bf16[32,2048]{1,0:T(8,128)(2,1)S(1)} %get-tuple-element.65), channel_id=1, source_target_pairs={{0,32},{1,9},{2,34},{3,11},{4,36},{5,13},{6,38},{7,15},{8,40},{9,1... | collective-permute-start | bytes 393224 | tf_op jit(solution)/shard_map/ppermute | solution.py:79
  224.0 11.1 %collective-permute-start.29 = (bf16[32,2048]{1,0:T(8,128)(2,1)S(1)}, bf16[32,2048]{1,0:T(8,128)(2,1)S(1)}, u32[]{:S(2)}, u32[]{:S(2)}) collective-permute-start(bf16[32,2048]{1,0:T(8,128)(2,1)S(1)} %get-tuple-element.64), channel_id=1, source_target_pairs={{0,96},{1,25},{2,98},{3,27},{4,100},{5,29},{6,102},{7,31},{8,104},... | collective-permute-start | bytes 393224 | tf_op jit(solution)/shard_map/ppermute | solution.py:79
  (30 other events, 162.8 us)
Sparse Core Ops, SparseCore 0:
  9.0 31.6 all-gather.2
  42.4 30.5 all-gather.4

commit v3 on v2

--- a/solution.py
+++ b/solution.py
@@ -12,7 +12,8 @@
 SEQUENCE_SLOTS = 128
 SIDE = 4
 TILE = 256
-AHEAD = 6
+AHEAD = 2
+WIDE = 512
 PIECES = 8
 PROJECT_BYTES = 12 * 1024 * 1024
 VMEM_BYTES = 52 * 1024 * 1024
@@ -189,22 +190,22 @@
 def gate_and_up(places, blocks, w_gate, w_up):
     depth, units = w_gate.shape
     rows = blocks[0].shape[0]
-    full = units // TILE
-    rest = units - full * TILE
+    full = units // WIDE
+    rest = units - full * WIDE
 
     def kernel(places, *refs):
         given, gate_ref, up_ref, outs = refs[:4], refs[4], refs[5], refs[6:8]
         lhs, tile_refs, sems = refs[8:]
 
         def copy(weight_ref, j, first):
-            at = pl.ds(pl.multiple_of(j * TILE, TILE), TILE)
+            at = pl.ds(pl.multiple_of(j * WIDE, WIDE), WIDE)
             return pltpu.make_async_copy(
                 weight_ref.at[:, at], tile_refs.at[first + j], sems.at[first + j]
             )
 
         def copy_rest(weight_ref, i):
             return pltpu.make_async_copy(
-                weight_ref.at[:, pl.ds(full * TILE, rest)],
+                weight_ref.at[:, pl.ds(full * WIDE, rest)],
                 tile_refs.at[2 * full, :, pl.ds(i * rest, rest)],
                 sems.at[2 * full + i],
             )
@@ -233,8 +234,8 @@
             def _():
                 copy(up_ref, j + AHEAD - full, full).start()
 
-            at = pl.multiple_of(j * TILE, TILE)
-            store(multiply(tile_refs[j]), pl.ds(at, TILE))
+            at = pl.multiple_of(j * WIDE, WIDE)
+            store(multiply(tile_refs[j]), pl.ds(at, WIDE))
 
         @pl.loop(0, full)
         def _(j):
@@ -249,14 +250,14 @@
                 copy_rest(gate_ref, 0).start()
                 copy_rest(up_ref, 1).start()
 
-            at = pl.multiple_of(units + j * TILE, 128)
-            store(multiply(tile_refs[full + j]), pl.ds(at, TILE))
+            at = pl.multiple_of(units + j * WIDE, 128)
+            store(multiply(tile_refs[full + j]), pl.ds(at, WIDE))
 
         copy_rest(gate_ref, 0).wait()
         copy_rest(up_ref, 1).wait()
-        product = multiply(tile_refs[2 * full])
-        store(product[:, :rest], pl.ds(full * TILE, rest))
-        store(product[:, rest:], pl.ds(units + full * TILE, rest))
+        product = multiply(tile_refs[2 * full, :, : 2 * rest])
+        store(product[:, :rest], pl.ds(full * WIDE, rest))
+        store(product[:, rest:], pl.ds(units + full * WIDE, rest))
 
     return pl.pallas_call(
         kernel,
@@ -264,7 +265,7 @@
         out_specs=[VMEM] * 2,
         scratch_shapes=[
             pltpu.VMEM((4 * rows, depth + 128), BF16),
-            pltpu.VMEM((2 * full + 1, depth, TILE), BF16),
+            pltpu.VMEM((2 * full + 1, depth, WIDE), BF16),
             pltpu.SemaphoreType.DMA((2 * full + 2,)),
         ],
         out_shape=[jax.ShapeDtypeStruct((2 * rows, 2 * units + 128), BF16)] * 2,

time: 247 us -> 246 us (level)
  no operation moved by 1% of the time
where the time goes in v3:
time: 246 us
  waiting for transfers between devices  110 us (45%)
  starting transfers between devices  50.1 us (20%)
  Pallas kernels  41.9 us (17%)
  local copies, waits for them, and re-layouts  20.4 us (8%)
  between operations  15.2 us (6%)
  other arithmetic  7.03 us (3%)
    ppermute x27, waiting for transfers between devices, move(): return lax.ppermute(array, BOTH, across(major, mask))  69.3 us
    ppermute x27, starting transfers between devices, move(): return lax.ppermute(array, BOTH, across(major, mask))  39.6 us
    pallas_call x2, Pallas kernels, gate_and_up(): pl.pallas_call(kernel, in_specs=[SMEM] + [VMEM] * 4 + [HBM] * 2, out_spec...  25.9 us
    unnamed x38, local copies, waits for them, and re-layouts  19 us
    pallas_call x3, Pallas kernels, project(): pl.pallas_call(kernel, in_specs=[SMEM] + [VMEM] * (len(blocks) + 1), out_...  14.4 us
    ppermute x2, waiting for transfers between devices, sum_over_x(): other = lax.ppermute(other, 'gy', across_x((1, 3)))  11.9 us
    ppermute x3, waiting for transfers between devices, gather_x(): lax.ppermute(jnp.concatenate([block, other]), 'gy', across_x((3, 1)))  11.3 us
    ppermute x3, waiting for transfers between devices, gather_x(): other = lax.ppermute(block, 'gy', across_x((1, 3)))  9.51 us
  transfers between devices with their start and end apart: 43, of which 30 were waited for; matrix products, arithmetic and copies ran while one was open for 3% of the time, Pallas kernels for 17%

profile of v3, /device:TPU:0, one launch (start us, length us, event | category | flops | bytes accessed | tf_op | source)
XLA Modules:
  0.0 246.0 jit_solution(16632320426893156251)
XLA Ops:
  17.5 2.9 %collective-permute-start.1 = (bf16[256,1024]{1,0:T(8,128)(2,1)S(1)}, bf16[256,1024]{1,0:T(8,128)(2,1)S(1)}, u32[]{:S(2)}, u32[]{:S(2)}) collective-permute-start(bf16[256,1024]{1,0:T(8,128)(2,1)S(1)} %pad_maximum_fusion.5), channel_id=1, source_target_pairs={{0,6},{1,3},{2,4},{3,1},{4,2},{5,7},{6,0},{7,5},{8,14},{9,11},{10,... | collective-permute-start | bytes 1572872 | tf_op jit(solution)/shard_map/ppermute | solution.py:92
  20.4 7.6 %collective-permute-done.1.refs_2_ = bf16[256,1024]{1,0:T(8,128)(2,1)S(1)} collective-permute-done((bf16[256,1024]{1,0:T(8,128)(2,1)S(1)}, bf16[256,1024]{1,0:T(8,128)(2,1)S(1)}, u32[]{:S(2)}, u32[]{:S(2)}) %collective-permute-start.1) | collective-permute-done | bytes 524320 | tf_op jit(solution)/shard_map/ppermute | solution.py:92
  30.8 3.4 %copy-done.8 = bf16[1024,2048]{1,0:T(8,128)(2,1)S(1)} copy-done((bf16[1024,2048]{1,0:T(8,128)(2,1)S(1)}, bf16[1024,2048]{1,0:T(8,128)(2,1)}, u32[]{:S(2)}) %copy-start.8) | copy-done | bytes 4194328
  34.3 5.2 %shard_map.110 = (bf16[256,2048]{1,0:T(8,128)(2,1)S(1)}, bf16[256,2048]{1,0:T(8,128)(2,1)S(1)}, bf16[256,2048]{1,0:T(8,128)(2,1)S(1)}, bf16[256,2048]{1,0:T(8,128)(2,1)S(1)}) custom-call(s32[16]{0:T(128)S(1)} %select_n.91.places, bf16[128,1024]{1,0:T(8,128)(2,1)S(1)} %copy.44.refs_0_, bf16[128,1024]{1,0:T(8,128)(2,1)S(1)} %collective-permute-done.refs_1_, ...), custom_call_target="tpu_custom_call" | custom-call | flops 4294967296 | bytes 4194304 | tf_op jit(solution)/shard_map/pallas_call | solution.py:177
  39.4 3.8 %collective-permute-start.3 = (bf16[256,2048]{1,0:T(8,128)(2,1)S(1)}, bf16[256,2048]{1,0:T(8,128)(2,1)S(1)}, u32[]{:S(2)}, u32[]{:S(2)}) collective-permute-start(bf16[256,2048]{1,0:T(8,128)(2,1)S(1)} %get-tuple-element.33), channel_id=1, source_target_pairs={{0,16},{1,65},{2,18},{3,67},{4,20},{5,69},{6,22},{7,71},{8,24},{9,... | collective-permute-start | bytes 3145736 | tf_op jit(solution)/shard_map/ppermute | solution.py:80
  44.8 11.3 %collective-permute-done.3 = bf16[256,2048]{1,0:T(8,128)(2,1)S(1)} collective-permute-done((bf16[256,2048]{1,0:T(8,128)(2,1)S(1)}, bf16[256,2048]{1,0:T(8,128)(2,1)S(1)}, u32[]{:S(2)}, u32[]{:S(2)}) %collective-permute-start.3) | collective-permute-done | bytes 1048608 | tf_op jit(solution)/shard_map/ppermute | solution.py:80
  56.1 12.8 %collective-permute-done.4 = bf16[256,2048]{1,0:T(8,128)(2,1)S(1)} collective-permute-done((bf16[256,2048]{1,0:T(8,128)(2,1)S(1)}, bf16[256,2048]{1,0:T(8,128)(2,1)S(1)}, u32[]{:S(2)}, u32[]{:S(2)}) %collective-permute-start.4) | collective-permute-done | bytes 1048608 | tf_op jit(solution)/shard_map/ppermute | solution.py:80
  71.1 3.1 %collective-permute-start.6 = (bf16[64,2048]{1,0:T(8,128)(2,1)}, bf16[64,2048]{1,0:T(8,128)(2,1)}, u32[]{:S(2)}, u32[]{:S(2)}) collective-permute-start(bf16[64,2048]{1,0:T(8,128)(2,1)} %get-tuple-element.60), channel_id=1, source_target_pairs={{0,64},{1,17},{2,66},{3,19},{4,68},{5,21},{6,70},{7,23},{8,72},{9,... | collective-permute-start | bytes 786440 | tf_op jit(solution)/shard_map/ppermute | solution.py:80
  75.3 4.0 %collective-permute-done.6 = bf16[64,2048]{1,0:T(8,128)(2,1)} collective-permute-done((bf16[64,2048]{1,0:T(8,128)(2,1)}, bf16[64,2048]{1,0:T(8,128)(2,1)}, u32[]{:S(2)}, u32[]{:S(2)}) %collective-permute-start.6) | collective-permute-done | bytes 262176 | tf_op jit(solution)/shard_map/ppermute | solution.py:80
  79.3 3.2 %collective-permute-done.7 = bf16[64,2048]{1,0:T(8,128)(2,1)} collective-permute-done((bf16[64,2048]{1,0:T(8,128)(2,1)}, bf16[64,2048]{1,0:T(8,128)(2,1)}, u32[]{:S(2)}, u32[]{:S(2)}) %collective-permute-start.7) | collective-permute-done | bytes 262176 | tf_op jit(solution)/shard_map/ppermute | solution.py:80
  88.4 2.8 %collective-permute-start.11 = (bf16[32,4224]{1,0:T(8,128)(2,1)S(1)}, bf16[32,4224]{1,0:T(8,128)(2,1)S(1)}, u32[]{:S(2)}, u32[]{:S(2)}) collective-permute-start(bf16[32,4224]{1,0:T(8,128)(2,1)S(1)} %fusion.8), channel_id=1, source_target_pairs={{0,64},{1,17},{2,66},{3,19},{4,68},{5,21},{6,70},{7,23},{8,72},{9,... | collective-permute-start | bytes 811016 | tf_op jit(solution)/shard_map/ppermute | solution.py:80
  93.7 4.9 %collective-permute-done.11 = bf16[32,4224]{1,0:T(8,128)(2,1)S(1)} collective-permute-done((bf16[32,4224]{1,0:T(8,128)(2,1)S(1)}, bf16[32,4224]{1,0:T(8,128)(2,1)S(1)}, u32[]{:S(2)}, u32[]{:S(2)}) %collective-permute-start.11) | collective-permute-done | bytes 270368 | tf_op jit(solution)/shard_map/ppermute | solution.py:80
  98.6 2.8 %collective-permute-done.12 = bf16[32,4224]{1,0:T(8,128)(2,1)S(1)} collective-permute-done((bf16[32,4224]{1,0:T(8,128)(2,1)S(1)}, bf16[32,4224]{1,0:T(8,128)(2,1)S(1)}, u32[]{:S(2)}, u32[]{:S(2)}) %collective-permute-start.12) | collective-permute-done | bytes 270368 | tf_op jit(solution)/shard_map/ppermute | solution.py:80
  102.5 3.1 %collective-permute-start.14 = (bf16[64,4224]{1,0:T(8,128)(2,1)S(1)}, bf16[64,4224]{1,0:T(8,128)(2,1)S(1)}, u32[]{:S(2)}, u32[]{:S(2)}) collective-permute-start(bf16[64,4224]{1,0:T(8,128)(2,1)S(1)} %pad_maximum_fusion.3.refs_0_), channel_id=1, source_target_pairs={{0,16},{1,65},{2,18},{3,67},{4,20},{5,69},{6,22},{7,71},{8,24},{9,... | collective-permute-start | bytes 1622024 | tf_op jit(solution)/shard_map/ppermute | solution.py:80
  106.4 4.1 %collective-permute-start.18 = (bf16[64,4224]{1,0:T(8,128)(2,1)S(1)}, bf16[64,4224]{1,0:T(8,128)(2,1)S(1)}, u32[]{:S(2)}, u32[]{:S(2)}) collective-permute-start(bf16[64,4224]{1,0:T(8,128)(2,1)S(1)} %pad_maximum_fusion.4.refs_0_), channel_id=1, source_target_pairs={{0,16},{1,65},{2,18},{3,67},{4,20},{5,69},{6,22},{7,71},{8,24},{9,... | collective-permute-start | bytes 1622024 | tf_op jit(solution)/shard_map/ppermute | solution.py:80
  113.5 5.3 %collective-permute-done.14.refs_2_ = bf16[64,4224]{1,0:T(8,128)(2,1)S(1)} collective-permute-done((bf16[64,4224]{1,0:T(8,128)(2,1)S(1)}, bf16[64,4224]{1,0:T(8,128)(2,1)S(1)}, u32[]{:S(2)}, u32[]{:S(2)}) %collective-permute-start.14) | collective-permute-done | bytes 540704 | tf_op jit(solution)/shard_map/ppermute | solution.py:80
  118.8 3.2 %collective-permute-done.15.refs_3_ = bf16[64,4224]{1,0:T(8,128)(2,1)} collective-permute-done((bf16[64,4224]{1,0:T(8,128)(2,1)S(1)}, bf16[64,4224]{1,0:T(8,128)(2,1)}, u32[]{:S(2)}, u32[]{:S(2)}) %collective-permute-start.15) | collective-permute-done | bytes 540704 | tf_op jit(solution)/shard_map/ppermute | solution.py:80
  122.1 12.9 %shard_map.111 = (bf16[128,3456]{1,0:T(8,128)(2,1)}, bf16[128,3456]{1,0:T(8,128)(2,1)}) custom-call(s32[4]{0:T(128)S(1)} %compare_select_fusion.2.places, bf16[64,4224]{1,0:T(8,128)(2,1)S(1)} %pad_maximum_fusion.3.refs_0_, bf16[64,4224]{1,0:T(8,128)(2,1)S(1)} %collective-permute-done.13.refs_1_, bf16[64,4224]{1,0:T(8,128)(2,1)S(1)} %collective-permute-done.14.refs_2_, ...), custom_call_target="tpu_custom_call" | custom-call | flops 6979321856 | bytes 27262976 | tf_op jit(solution)/shard_map/pallas_call | solution.py:262
  135.0 2.8 %collective-permute-start.16 = (bf16[128,3456]{1,0:T(8,128)(2,1)}, bf16[128,3456]{1,0:T(8,128)(2,1)S(1)}, u32[]{:S(2)}, u32[]{:S(2)}) collective-permute-start(bf16[128,3456]{1,0:T(8,128)(2,1)} %get-tuple-element.37), channel_id=1, source_target_pairs={{0,6},{1,3},{2,4},{3,1},{4,2},{5,7},{6,0},{7,5},{8,14},{9,11},{10,... | collective-permute-start | bytes 2654216 | tf_op jit(solution)/shard_map/ppermute | solution.py:281
  137.8 13.0 %shard_map.112 = (bf16[128,3456]{1,0:T(8,128)(2,1)}, bf16[128,3456]{1,0:T(8,128)(2,1)}) custom-call(s32[4]{0:T(128)S(1)} %compare_select_fusion.2.places, bf16[64,4224]{1,0:T(8,128)(2,1)S(1)} %pad_maximum_fusion.4.refs_0_, bf16[64,4224]{1,0:T(8,128)(2,1)S(1)} %collective-permute-done.17.refs_1_, bf16[64,4224]{1,0:T(8,128)(2,1)S(1)} %collective-permute-done.18.refs_2_, ...), custom_call_target="tpu_custom_call" | custom-call | flops 6979321856 | bytes 27262976 | tf_op jit(solution)/shard_map/pallas_call | solution.py:262
  153.4 2.9 %copy-done.2 = bf16[1664,2048]{1,0:T(8,128)(2,1)S(1)} copy-done((bf16[1664,2048]{1,0:T(8,128)(2,1)S(1)}, bf16[1664,2048]{1,0:T(8,128)(2,1)}, u32[]{:S(2)}) %copy-start.2) | copy-done | bytes 6815768
  160.3 4.7 %collective-permute-done.20 = bf16[64,3456]{1,0:T(8,128)(2,1)S(1)} collective-permute-done((bf16[64,3456]{1,0:T(8,128)(2,1)S(1)}, bf16[64,3456]{1,0:T(8,128)(2,1)S(1)}, u32[]{:S(2)}, u32[]{:S(2)}) %collective-permute-start.20) | collective-permute-done | bytes 442400 | tf_op jit(solution)/shard_map/ppermute | solution.py:283
  165.6 3.1 %collective-permute-done.30 = bf16[128,3456]{1,0:T(8,128)(2,1)S(1)} collective-permute-done((bf16[128,3456]{1,0:T(8,128)(2,1)}, bf16[128,3456]{1,0:T(8,128)(2,1)S(1)}, u32[]{:S(2)}, u32[]{:S(2)}) %collective-permute-start.30) | collective-permute-done | bytes 884768 | tf_op jit(solution)/shard_map/ppermute | solution.py:281
  169.8 3.6 %collective-permute-done.21.refs_1_ = bf16[64,1664]{1,0:T(8,128)(2,1)S(1)} collective-permute-done((bf16[64,1664]{1,0:T(8,128)(2,1)S(1)}, bf16[64,1664]{1,0:T(8,128)(2,1)S(1)}, u32[]{:S(2)}, u32[]{:S(2)}) %collective-permute-start.21) | collective-permute-done | bytes 213024 | tf_op jit(solution)/shard_map/ppermute | solution.py:89
  173.5 7.2 %collective-permute-done.31 = bf16[64,3456]{1,0:T(8,128)(2,1)S(1)} collective-permute-done((bf16[64,3456]{1,0:T(8,128)(2,1)S(1)}, bf16[64,3456]{1,0:T(8,128)(2,1)S(1)}, u32[]{:S(2)}, u32[]{:S(2)}) %collective-permute-start.31) | collective-permute-done | bytes 442400 | tf_op jit(solution)/shard_map/ppermute | solution.py:283
  183.4 5.8 %collective-permute-done.32.refs_1_ = bf16[64,1664]{1,0:T(8,128)(2,1)S(1)} collective-permute-done((bf16[64,1664]{1,0:T(8,128)(2,1)S(1)}, bf16[64,1664]{1,0:T(8,128)(2,1)S(1)}, u32[]{:S(2)}, u32[]{:S(2)}) %collective-permute-start.32) | collective-permute-done | bytes 213024 | tf_op jit(solution)/shard_map/ppermute | solution.py:89
  190.1 2.9 %copy-done.4 = bf16[1664,2048]{1,0:T(8,128)(2,1)S(1)} copy-done((bf16[1664,2048]{1,0:T(8,128)(2,1)S(1)}, bf16[1664,2048]{1,0:T(8,128)(2,1)}, u32[]{:S(2)}) %copy-start.4) | copy-done | bytes 6815768
  193.0 4.6 %shard_map.114 = (bf16[128,2048]{1,0:T(8,128)(2,1)S(1)}, bf16[128,2048]{1,0:T(8,128)(2,1)S(1)}, bf16[128,2048]{1,0:T(8,128)(2,1)S(1)}, bf16[128,2048]{1,0:T(8,128)(2,1)S(1)}) custom-call(s32[32]{0:T(128)S(1)} %reshape.426.places, bf16[64,1664]{1,0:T(8,128)(2,1)S(1)} %multiply_convert_fusion.1.refs_0_, bf16[64,1664]{1,0:T(8,128)(2,1)S(1)} %collective-permute-done.21.refs_1_, ...), custom_call_target="tpu_custom_call" | custom-call | flops 3489660928 | bytes 6815744 | tf_op jit(solution)/shard_map/pallas_call | solution.py:177
  200.9 2.9 %collective-permute-start.26 = (bf16[128,2048]{1,0:T(8,128)(2,1)S(1)}, bf16[128,2048]{1,0:T(8,128)(2,1)S(1)}, u32[]{:S(2)}, u32[]{:S(2)}) collective-permute-start(bf16[128,2048]{1,0:T(8,128)(2,1)S(1)} %get-tuple-element.45), channel_id=1, source_target_pairs={{0,24},{1,97},{2,26},{3,99},{4,28},{5,101},{6,30},{7,103},{8,16},{... | collective-permute-start | bytes 1572872 | tf_op jit(solution)/shard_map/ppermute | solution.py:80
  203.8 4.7 %shard_map.115 = (bf16[128,2048]{1,0:T(8,128)(2,1)S(1)}, bf16[128,2048]{1,0:T(8,128)(2,1)S(1)}, bf16[128,2048]{1,0:T(8,128)(2,1)S(1)}, bf16[128,2048]{1,0:T(8,128)(2,1)S(1)}) custom-call(s32[32]{0:T(128)S(1)} %reshape.426.places, bf16[64,1664]{1,0:T(8,128)(2,1)S(1)} %fusion.6.refs_0_, bf16[64,1664]{1,0:T(8,128)(2,1)S(1)} %collective-permute-done.32.refs_1_, ...), custom_call_target="tpu_custom_call" | custom-call | flops 3489660928 | bytes 6815744 | tf_op jit(solution)/shard_map/pallas_call | solution.py:177
  217.7 5.6 %collective-permute-done.35 = bf16[128,2048]{1,0:T(8,128)(2,1)S(1)} collective-permute-done((bf16[128,2048]{1,0:T(8,128)(2,1)S(1)}, bf16[128,2048]{1,0:T(8,128)(2,1)S(1)}, u32[]{:S(2)}, u32[]{:S(2)}) %collective-permute-start.35) | collective-permute-done | bytes 524320 | tf_op jit(solution)/shard_map/ppermute | solution.py:80
  223.9 4.0 %collective-permute-done.36 = bf16[128,2048]{1,0:T(8,128)(2,1)S(1)} collective-permute-done((bf16[128,2048]{1,0:T(8,128)(2,1)S(1)}, bf16[128,2048]{1,0:T(8,128)(2,1)S(1)}, u32[]{:S(2)}, u32[]{:S(2)}) %collective-permute-start.36) | collective-permute-done | bytes 524320 | tf_op jit(solution)/shard_map/ppermute | solution.py:80
  (164 shorter events, 66.7 us)
Async XLA Ops:
  6.5 115.5 %all-gather.3.cloned.1.call-start = ((), (), s32[]{:S(2)}) async-start(), calls=%async_computation | async-start | bytes 20447232 | tf_op jit(solution)/shard_map/all_gather | solution.py:301
  7.3 114.8 %all-gather.5.cloned.1.call-start = ((), (), s32[]{:S(2)}) async-start(), calls=%async_computation.1 | async-start | bytes 20447232 | tf_op jit(solution)/shard_map/all_gather | solution.py:302
  17.5 10.5 %collective-permute-start.1 = (bf16[256,1024]{1,0:T(8,128)(2,1)S(1)}, bf16[256,1024]{1,0:T(8,128)(2,1)S(1)}, u32[]{:S(2)}, u32[]{:S(2)}) collective-permute-start(bf16[256,1024]{1,0:T(8,128)(2,1)S(1)} %pad_maximum_fusion.5), channel_id=1, source_target_pairs={{0,6},{1,3},{2,4},{3,1},{4,2},{5,7},{6,0},{7,5},{8,14},{9,11},{10,... | collective-permute-start | bytes 1572872 | tf_op jit(solution)/shard_map/ppermute | solution.py:92
  39.4 16.6 %collective-permute-start.3 = (bf16[256,2048]{1,0:T(8,128)(2,1)S(1)}, bf16[256,2048]{1,0:T(8,128)(2,1)S(1)}, u32[]{:S(2)}, u32[]{:S(2)}) collective-permute-start(bf16[256,2048]{1,0:T(8,128)(2,1)S(1)} %get-tuple-element.33), channel_id=1, source_target_pairs={{0,16},{1,65},{2,18},{3,67},{4,20},{5,69},{6,22},{7,71},{8,24},{9,... | collective-permute-start | bytes 3145736 | tf_op jit(solution)/shard_map/ppermute | solution.py:80
  43.2 25.6 %collective-permute-start.4 = (bf16[256,2048]{1,0:T(8,128)(2,1)S(1)}, bf16[256,2048]{1,0:T(8,128)(2,1)S(1)}, u32[]{:S(2)}, u32[]{:S(2)}) collective-permute-start(bf16[256,2048]{1,0:T(8,128)(2,1)S(1)} %get-tuple-element.34), channel_id=1, source_target_pairs={{0,8},{1,33},{2,10},{3,35},{4,12},{5,37},{6,14},{7,39},{8,0},{9,41... | collective-permute-start | bytes 3145736 | tf_op jit(solution)/shard_map/ppermute | solution.py:80
  44.8 24.1 %collective-permute-start.5 = (bf16[256,2048]{1,0:T(8,128)(2,1)S(1)}, bf16[256,2048]{1,0:T(8,128)(2,1)S(1)}, u32[]{:S(2)}, u32[]{:S(2)}) collective-permute-start(bf16[256,2048]{1,0:T(8,128)(2,1)S(1)} %get-tuple-element.35), channel_id=1, source_target_pairs={{0,24},{1,97},{2,26},{3,99},{4,28},{5,101},{6,30},{7,103},{8,16},{... | collective-permute-start | bytes 3145736 | tf_op jit(solution)/shard_map/ppermute | solution.py:80
  71.1 8.2 %collective-permute-start.6 = (bf16[64,2048]{1,0:T(8,128)(2,1)}, bf16[64,2048]{1,0:T(8,128)(2,1)}, u32[]{:S(2)}, u32[]{:S(2)}) collective-permute-start(bf16[64,2048]{1,0:T(8,128)(2,1)} %get-tuple-element.60), channel_id=1, source_target_pairs={{0,64},{1,17},{2,66},{3,19},{4,68},{5,21},{6,70},{7,23},{8,72},{9,... | collective-permute-start | bytes 786440 | tf_op jit(solution)/shard_map/ppermute | solution.py:80
  74.3 8.2 %collective-permute-start.7 = (bf16[64,2048]{1,0:T(8,128)(2,1)}, bf16[64,2048]{1,0:T(8,128)(2,1)}, u32[]{:S(2)}, u32[]{:S(2)}) collective-permute-start(bf16[64,2048]{1,0:T(8,128)(2,1)} %get-tuple-element.62), channel_id=1, source_target_pairs={{0,32},{1,9},{2,34},{3,11},{4,36},{5,13},{6,38},{7,15},{8,40},{9,1... | collective-permute-start | bytes 786440 | tf_op jit(solution)/shard_map/ppermute | solution.py:80
  88.4 10.2 %collective-permute-start.11 = (bf16[32,4224]{1,0:T(8,128)(2,1)S(1)}, bf16[32,4224]{1,0:T(8,128)(2,1)S(1)}, u32[]{:S(2)}, u32[]{:S(2)}) collective-permute-start(bf16[32,4224]{1,0:T(8,128)(2,1)S(1)} %fusion.8), channel_id=1, source_target_pairs={{0,64},{1,17},{2,66},{3,19},{4,68},{5,21},{6,70},{7,23},{8,72},{9,... | collective-permute-start | bytes 811016 | tf_op jit(solution)/shard_map/ppermute | solution.py:80
  91.1 10.2 %collective-permute-start.12 = (bf16[32,4224]{1,0:T(8,128)(2,1)S(1)}, bf16[32,4224]{1,0:T(8,128)(2,1)S(1)}, u32[]{:S(2)}, u32[]{:S(2)}) collective-permute-start(bf16[32,4224]{1,0:T(8,128)(2,1)S(1)} %fusion.8), channel_id=1, source_target_pairs={{0,96},{1,25},{2,98},{3,27},{4,100},{5,29},{6,102},{7,31},{8,104},... | collective-permute-start | bytes 811016 | tf_op jit(solution)/shard_map/ppermute | solution.py:80
  101.4 9.4 %collective-permute-start.13 = (bf16[64,4224]{1,0:T(8,128)(2,1)S(1)}, bf16[64,4224]{1,0:T(8,128)(2,1)S(1)}, u32[]{:S(2)}, u32[]{:S(2)}) collective-permute-start(bf16[64,4224]{1,0:T(8,128)(2,1)S(1)} %pad_maximum_fusion.3.refs_0_), channel_id=1, source_target_pairs={{0,8},{1,33},{2,10},{3,35},{4,12},{5,37},{6,14},{7,39},{8,0},{9,41... | collective-permute-start | bytes 1622024 | tf_op jit(solution)/shard_map/ppermute | solution.py:80
  102.5 16.3 %collective-permute-start.14 = (bf16[64,4224]{1,0:T(8,128)(2,1)S(1)}, bf16[64,4224]{1,0:T(8,128)(2,1)S(1)}, u32[]{:S(2)}, u32[]{:S(2)}) collective-permute-start(bf16[64,4224]{1,0:T(8,128)(2,1)S(1)} %pad_maximum_fusion.3.refs_0_), channel_id=1, source_target_pairs={{0,16},{1,65},{2,18},{3,67},{4,20},{5,69},{6,22},{7,71},{8,24},{9,... | collective-permute-start | bytes 1622024 | tf_op jit(solution)/shard_map/ppermute | solution.py:80
  105.6 16.5 %collective-permute-start.15 = (bf16[64,4224]{1,0:T(8,128)(2,1)S(1)}, bf16[64,4224]{1,0:T(8,128)(2,1)}, u32[]{:S(2)}, u32[]{:S(2)}) collective-permute-start(bf16[64,4224]{1,0:T(8,128)(2,1)S(1)} %pad_maximum_fusion.3.refs_0_), channel_id=1, source_target_pairs={{0,24},{1,97},{2,26},{3,99},{4,28},{5,101},{6,30},{7,103},{8,16},{... | collective-permute-start | bytes 1622024 | tf_op jit(solution)/shard_map/ppermute | solution.py:80
  106.3 31.6 %collective-permute-start.17 = (bf16[64,4224]{1,0:T(8,128)(2,1)S(1)}, bf16[64,4224]{1,0:T(8,128)(2,1)S(1)}, u32[]{:S(2)}, u32[]{:S(2)}) collective-permute-start(bf16[64,4224]{1,0:T(8,128)(2,1)S(1)} %pad_maximum_fusion.4.refs_0_), channel_id=1, source_target_pairs={{0,8},{1,33},{2,10},{3,35},{4,12},{5,37},{6,14},{7,39},{8,0},{9,41... | collective-permute-start | bytes 1622024 | tf_op jit(solution)/shard_map/ppermute | solution.py:80
  106.4 31.5 %collective-permute-start.18 = (bf16[64,4224]{1,0:T(8,128)(2,1)S(1)}, bf16[64,4224]{1,0:T(8,128)(2,1)S(1)}, u32[]{:S(2)}, u32[]{:S(2)}) collective-permute-start(bf16[64,4224]{1,0:T(8,128)(2,1)S(1)} %pad_maximum_fusion.4.refs_0_), channel_id=1, source_target_pairs={{0,16},{1,65},{2,18},{3,67},{4,20},{5,69},{6,22},{7,71},{8,24},{9,... | collective-permute-start | bytes 1622024 | tf_op jit(solution)/shard_map/ppermute | solution.py:80
  110.9 27.0 %collective-permute-start.19 = (bf16[64,4224]{1,0:T(8,128)(2,1)S(1)}, bf16[64,4224]{1,0:T(8,128)(2,1)}, u32[]{:S(2)}, u32[]{:S(2)}) collective-permute-start(bf16[64,4224]{1,0:T(8,128)(2,1)S(1)} %pad_maximum_fusion.4.refs_0_), channel_id=1, source_target_pairs={{0,24},{1,97},{2,26},{3,99},{4,28},{5,101},{6,30},{7,103},{8,16},{... | collective-permute-start | bytes 1622024 | tf_op jit(solution)/shard_map/ppermute | solution.py:80
  135.0 15.9 %collective-permute-start.16 = (bf16[128,3456]{1,0:T(8,128)(2,1)}, bf16[128,3456]{1,0:T(8,128)(2,1)S(1)}, u32[]{:S(2)}, u32[]{:S(2)}) collective-permute-start(bf16[128,3456]{1,0:T(8,128)(2,1)} %get-tuple-element.37), channel_id=1, source_target_pairs={{0,6},{1,3},{2,4},{3,1},{4,2},{5,7},{6,0},{7,5},{8,14},{9,11},{10,... | collective-permute-start | bytes 2654216 | tf_op jit(solution)/shard_map/ppermute | solution.py:281
  151.9 13.1 %collective-permute-start.20 = (bf16[64,3456]{1,0:T(8,128)(2,1)S(1)}, bf16[64,3456]{1,0:T(8,128)(2,1)S(1)}, u32[]{:S(2)}, u32[]{:S(2)}) collective-permute-start(bf16[64,3456]{1,0:T(8,128)(2,1)S(1)} %add_convert_fusion.1), channel_id=1, source_target_pairs={{0,2},{1,7},{2,0},{3,5},{4,6},{5,3},{6,4},{7,1},{8,10},{9,15},{10,... | collective-permute-start | bytes 1327112 | tf_op jit(solution)/shard_map/ppermute | solution.py:283
  151.9 16.8 %collective-permute-start.30 = (bf16[128,3456]{1,0:T(8,128)(2,1)}, bf16[128,3456]{1,0:T(8,128)(2,1)S(1)}, u32[]{:S(2)}, u32[]{:S(2)}) collective-permute-start(bf16[128,3456]{1,0:T(8,128)(2,1)} %get-tuple-element.38), channel_id=1, source_target_pairs={{0,6},{1,3},{2,4},{3,1},{4,2},{5,7},{6,0},{7,5},{8,14},{9,11},{10,... | collective-permute-start | bytes 2654216 | tf_op jit(solution)/shard_map/ppermute | solution.py:281
  165.5 7.9 %collective-permute-start.21 = (bf16[64,1664]{1,0:T(8,128)(2,1)S(1)}, bf16[64,1664]{1,0:T(8,128)(2,1)S(1)}, u32[]{:S(2)}, u32[]{:S(2)}) collective-permute-start(bf16[64,1664]{1,0:T(8,128)(2,1)S(1)} %multiply_convert_fusion.1.refs_0_), channel_id=1, source_target_pairs={{0,2},{1,7},{2,0},{3,5},{4,6},{5,3},{6,4},{7,1},{8,10},{9,15},{10,... | collective-permute-start | bytes 638984 | tf_op jit(solution)/shard_map/ppermute | solution.py:89
  168.8 11.9 %collective-permute-start.31 = (bf16[64,3456]{1,0:T(8,128)(2,1)S(1)}, bf16[64,3456]{1,0:T(8,128)(2,1)S(1)}, u32[]{:S(2)}, u32[]{:S(2)}) collective-permute-start(bf16[64,3456]{1,0:T(8,128)(2,1)S(1)} %add_convert_fusion), channel_id=1, source_target_pairs={{0,2},{1,7},{2,0},{3,5},{4,6},{5,3},{6,4},{7,1},{8,10},{9,15},{10,... | collective-permute-start | bytes 1327112 | tf_op jit(solution)/shard_map/ppermute | solution.py:283
  173.4 9.4 %collective-permute-start.22 = (bf16[128,1664]{1,0:T(8,128)(2,1)S(1)}, bf16[128,1664]{1,0:T(8,128)(2,1)S(1)}, u32[]{:S(2)}, u32[]{:S(2)}) collective-permute-start(bf16[128,1664]{1,0:T(8,128)(2,1)S(1)} %pad_maximum_fusion.6), channel_id=1, source_target_pairs={{0,6},{1,3},{2,4},{3,1},{4,2},{5,7},{6,0},{7,5},{8,14},{9,11},{10,... | collective-permute-start | bytes 1277960 | tf_op jit(solution)/shard_map/ppermute | solution.py:92
  189.9 9.5 %collective-permute-start.33 = (bf16[128,1664]{1,0:T(8,128)(2,1)}, bf16[128,1664]{1,0:T(8,128)(2,1)S(1)}, u32[]{:S(2)}, u32[]{:S(2)}) collective-permute-start(bf16[128,1664]{1,0:T(8,128)(2,1)} %pad_maximum_fusion.7), channel_id=1, source_target_pairs={{0,6},{1,3},{2,4},{3,1},{4,2},{5,7},{6,0},{7,5},{8,14},{9,11},{10,... | collective-permute-start | bytes 1277960 | tf_op jit(solution)/shard_map/ppermute | solution.py:92
  199.6 10.9 %collective-permute-start.24 = (bf16[128,2048]{1,0:T(8,128)(2,1)S(1)}, bf16[128,2048]{1,0:T(8,128)(2,1)S(1)}, u32[]{:S(2)}, u32[]{:S(2)}) collective-permute-start(bf16[128,2048]{1,0:T(8,128)(2,1)S(1)} %get-tuple-element.43), channel_id=1, source_target_pairs={{0,16},{1,65},{2,18},{3,67},{4,20},{5,69},{6,22},{7,71},{8,24},{9,... | collective-permute-start | bytes 1572872 | tf_op jit(solution)/shard_map/ppermute | solution.py:80
  199.7 14.0 %collective-permute-start.25 = (bf16[128,2048]{1,0:T(8,128)(2,1)S(1)}, bf16[128,2048]{1,0:T(8,128)(2,1)S(1)}, u32[]{:S(2)}, u32[]{:S(2)}) collective-permute-start(bf16[128,2048]{1,0:T(8,128)(2,1)S(1)} %get-tuple-element.44), channel_id=1, source_target_pairs={{0,8},{1,33},{2,10},{3,35},{4,12},{5,37},{6,14},{7,39},{8,0},{9,41... | collective-permute-start | bytes 1572872 | tf_op jit(solution)/shard_map/ppermute | solution.py:80
  200.9 15.1 %collective-permute-start.26 = (bf16[128,2048]{1,0:T(8,128)(2,1)S(1)}, bf16[128,2048]{1,0:T(8,128)(2,1)S(1)}, u32[]{:S(2)}, u32[]{:S(2)}) collective-permute-start(bf16[128,2048]{1,0:T(8,128)(2,1)S(1)} %get-tuple-element.45), channel_id=1, source_target_pairs={{0,24},{1,97},{2,26},{3,99},{4,28},{5,101},{6,30},{7,103},{8,16},{... | collective-permute-start | bytes 1572872 | tf_op jit(solution)/shard_map/ppermute | solution.py:80
  208.5 14.9 %collective-permute-start.35 = (bf16[128,2048]{1,0:T(8,128)(2,1)S(1)}, bf16[128,2048]{1,0:T(8,128)(2,1)S(1)}, u32[]{:S(2)}, u32[]{:S(2)}) collective-permute-start(bf16[128,2048]{1,0:T(8,128)(2,1)S(1)} %get-tuple-element.52), channel_id=1, source_target_pairs={{0,16},{1,65},{2,18},{3,67},{4,20},{5,69},{6,22},{7,71},{8,24},{9,... | collective-permute-start | bytes 1572872 | tf_op jit(solution)/shard_map/ppermute | solution.py:80
  208.7 19.2 %collective-permute-start.36 = (bf16[128,2048]{1,0:T(8,128)(2,1)S(1)}, bf16[128,2048]{1,0:T(8,128)(2,1)S(1)}, u32[]{:S(2)}, u32[]{:S(2)}) collective-permute-start(bf16[128,2048]{1,0:T(8,128)(2,1)S(1)} %get-tuple-element.53), channel_id=1, source_target_pairs={{0,8},{1,33},{2,10},{3,35},{4,12},{5,37},{6,14},{7,39},{8,0},{9,41... | collective-permute-start | bytes 1572872 | tf_op jit(solution)/shard_map/ppermute | solution.py:80
  210.5 19.6 %collective-permute-start.37 = (bf16[128,2048]{1,0:T(8,128)(2,1)S(1)}, bf16[128,2048]{1,0:T(8,128)(2,1)S(1)}, u32[]{:S(2)}, u32[]{:S(2)}) collective-permute-start(bf16[128,2048]{1,0:T(8,128)(2,1)S(1)} %get-tuple-element.54), channel_id=1, source_target_pairs={{0,24},{1,97},{2,26},{3,99},{4,28},{5,101},{6,30},{7,103},{8,16},{... | collective-permute-start | bytes 1572872 | tf_op jit(solution)/shard_map/ppermute | solution.py:80
  216.3 15.5 %collective-permute-start.27 = (bf16[32,2048]{1,0:T(8,128)(2,1)S(1)}, bf16[32,2048]{1,0:T(8,128)(2,1)S(1)}, u32[]{:S(2)}, u32[]{:S(2)}) collective-permute-start(bf16[32,2048]{1,0:T(8,128)(2,1)S(1)} %get-tuple-element.63), channel_id=1, source_target_pairs={{0,64},{1,17},{2,66},{3,19},{4,68},{5,21},{6,70},{7,23},{8,72},{9,... | collective-permute-start | bytes 393224 | tf_op jit(solution)/shard_map/ppermute | solution.py:80
  216.6 17.9 %collective-permute-start.28 = (bf16[32,2048]{1,0:T(8,128)(2,1)S(1)}, bf16[32,2048]{1,0:T(8,128)(2,1)S(1)}, u32[]{:S(2)}, u32[]{:S(2)}) collective-permute-start(bf16[32,2048]{1,0:T(8,128)(2,1)S(1)} %get-tuple-element.65), channel_id=1, source_target_pairs={{0,32},{1,9},{2,34},{3,11},{4,36},{5,13},{6,38},{7,15},{8,40},{9,1... | collective-permute-start | bytes 393224 | tf_op jit(solution)/shard_map/ppermute | solution.py:80
  223.4 11.1 %collective-permute-start.29 = (bf16[32,2048]{1,0:T(8,128)(2,1)S(1)}, bf16[32,2048]{1,0:T(8,128)(2,1)S(1)}, u32[]{:S(2)}, u32[]{:S(2)}) collective-permute-start(bf16[32,2048]{1,0:T(8,128)(2,1)S(1)} %get-tuple-element.64), channel_id=1, source_target_pairs={{0,96},{1,25},{2,98},{3,27},{4,100},{5,29},{6,102},{7,31},{8,104},... | collective-permute-start | bytes 393224 | tf_op jit(solution)/shard_map/ppermute | solution.py:80
  (30 other events, 161.6 us)
Sparse Core Ops, SparseCore 0:
  9.0 31.6 all-gather.2
  42.4 30.5 all-gather.4
